TPU v7x, 32 devices: a whole 2x2x4 slice. The times are simulated.
32 devices in a mesh: band: 32 (over z, y, x, core).
Axes of the slice: x: 2, y: 2, z: 4, core: 2. Of those that a mesh axis runs over, the one named last changes fastest.
Arguments:
- grid_features: bfloat16 [98304, 1024], P('band'), may hold values from -6 to 6
- mesh_features: bfloat16 [8192, 1024], P('band'), may hold values from -102 to 102
- sources: int32 [8192, 12], P('band'), may hold values from 0 to 98303, as said below
- window_shift: int32 [1], replicated, may hold values from 1 to 127
- w_query: bfloat16 [1024, 1024], replicated, may hold values from -0.1875 to 0.1875
- w_grid_kv: bfloat16 [1024, 2048], replicated, may hold values from -0.1875 to 0.1875
- w_enc_out: bfloat16 [1024, 1024], replicated, may hold values from -0.1875 to 0.1875
- norm_gain: float32 [1024], replicated, may hold values from 0.5 to 1.5
- w_win_qkv: bfloat16 [1024, 3072], replicated, may hold values from -0.1875 to 0.1875
- w_win_out: bfloat16 [1024, 1024], replicated, may hold values from -0.1875 to 0.1875
- head_scale: float32 [16], replicated, may hold values from 0.5 to 48
Outputs:
- mixed: bfloat16 [8192, 1024], P('band')
Inputs may be any that keep to these rules, and one draw needn't show every extreme that they name: `sources`: mesh node m of band b = m // 256 names grid points of its own band, b * 3072 to (b + 1) * 3072 - 1, unless it is among the first or the last 16 nodes of its band; those name points from b * 3072 - 384 to (b + 1) * 3072 + 383, cut to the grid, the first ones never above their own band and the last ones never below it. In every band both ends of that range are named where they lie in the grid.
All inputs are finite; a program needn't handle non-finite values.
Results may differ from a plain program's by a relative error of at most 0.01.
Values may be sent and summed in bfloat16 or wider, within the bound.
No kernel may reach another device: no remote copies, remote signals or barrier semaphores. Data moves between devices by JAX's collectives and lax.ppermute only.
A program may use at most 192 MiB of HBM per device.

v0:
```python
import jax
import jax.numpy as jnp
from jax import lax
from jax.experimental import pallas as pl
from jax.experimental.pallas import tpu as pltpu
from jax.sharding import PartitionSpec as P

WIN = 128
REACH = 384
RIM = 16
HEAD = 64
QUAD = 256
LANES = 128
NEG = -1e30
HALO_FLOPS = 10**10
HALO_BYTES = 3 * 10**7

BF16 = jnp.bfloat16
F32 = jnp.float32


def dot(a, b):
    return jnp.dot(a, b, preferred_element_type=F32)


def dot_t(a, b):
    return lax.dot_general(a, b, (((1,), (1,)), ((), ())), preferred_element_type=F32)


def layer_norm(mid, gain):
    wide = mid.astype(F32)
    center = jnp.mean(wide, axis=-1, keepdims=True)
    spread = jnp.mean((wide - center) ** 2, axis=-1, keepdims=True)
    return ((wide - center) / jnp.sqrt(spread + 1e-05) * gain).astype(BF16)


def count_edges(rel, start, cols):
    nodes, edge_count = rel.shape
    row = lax.broadcasted_iota(jnp.int32, (nodes, cols), 1) + start
    total = jnp.zeros((nodes, cols), F32)
    for e in range(edge_count):
        total += (rel[:, e : e + 1] == row).astype(F32)
    return total


def by_node(values):
    return values.reshape(values.shape[0] // RIM, RIM, values.shape[1])


def masked_scores(queries, rows, count):
    return by_node(dot_t(queries, rows)) + jnp.where(count > 0, 0.0, NEG)[None]


def row_weights(queries, rows, count):
    scores = masked_scores(queries, rows, count)
    top = jnp.max(scores, axis=-1, keepdims=True)
    grown = jnp.exp(scores - top) * count[None]
    weights = grown / jnp.sum(grown, axis=-1, keepdims=True)
    return weights.reshape(queries.shape[0], rows.shape[0]).astype(BF16)


def attend_all(queries, rel, rows_ref, total_ref):
    blocks = rows_ref.shape[0] // WIN
    heads = queries.shape[0] // RIM

    def block(i):
        at = pl.multiple_of(i * WIN, WIN)
        rows = rows_ref[pl.ds(at, WIN), :]
        count = count_edges(rel, at, WIN)
        return rows, count, masked_scores(queries, rows, count)

    def find(i, carry):
        top, size = carry
        _, count, scores = block(i)
        new = jnp.maximum(top, jnp.max(scores, axis=-1, keepdims=True))
        part = jnp.sum(jnp.exp(scores - new) * count[None], axis=-1, keepdims=True)
        return new, size * jnp.exp(top - new) + part

    start = (jnp.full((heads, RIM, 1), NEG, F32), jnp.zeros((heads, RIM, 1), F32))
    top, size = lax.fori_loop(0, blocks, find, start)
    total_ref[...] = jnp.zeros(total_ref.shape, F32)

    def add(i, carry):
        rows, count, scores = block(i)
        weights = jnp.exp(scores - top) * count[None] / size
        total_ref[...] += dot(weights.reshape(heads * RIM, WIN).astype(BF16), rows)
        return carry

    lax.fori_loop(0, blocks, add, 0)
    return total_ref[...].astype(BF16)


def project_heads(pool, w_ref, out_ref, quad):
    per, rows, width = pool.shape
    cols = pl.ds(pl.multiple_of(quad * QUAD, QUAD), QUAD)
    wide = dot(pool.reshape(per * rows, width), w_ref[:, cols])
    head = lax.broadcasted_iota(jnp.int32, (rows, QUAD), 1) // HEAD
    total = wide[:rows]
    for j in range(1, per):
        total = jnp.where(head == j, wide[j * rows : (j + 1) * rows], total)
    out_ref[:, cols] = total.astype(BF16)


def halo_kernel(first_in, last_in, first_ref, last_ref):
    first_ref[...] = first_in[...]
    last_ref[...] = last_in[...]


def interior_kernel(
    rel_ref, x_hbm, mesh_ref, wq_hbm, wkv_hbm, we_hbm, gain_ref,
    mid_ref, norm_ref, qrim_ref,
    x_ref, wq_ref, wkv_ref, we_ref,
    pool, pooled, qs, gathered, total_ref, begin_ref, fits_ref, sems,
):
    width = mesh_ref.shape[1]
    key_cols, value_cols = pl.ds(0, width), pl.ds(width, width)
    copies = [
        pltpu.make_async_copy(source, target, sems.at[i])
        for i, (source, target) in enumerate(
            (
                (wq_hbm, wq_ref),
                (wkv_hbm.at[:, key_cols], wkv_ref.at[:, key_cols]),
                (x_hbm, x_ref),
                (wkv_hbm.at[:, value_cols], wkv_ref.at[:, value_cols]),
                (we_hbm, we_ref),
            )
        )
    ]
    for copy in copies:
        copy.start()
    heads, mesh_rows, width = pool.shape
    grid_rows = x_ref.shape[0]
    quads = width // QUAD
    groups = mesh_rows // RIM
    for group in range(1, groups - 1):
        rel = rel_ref[group * RIM : (group + 1) * RIM, :].astype(F32)
        low = jnp.min(rel).astype(jnp.int32)
        high = jnp.max(rel).astype(jnp.int32)
        begin = jnp.clip(low // 16 * 16, 0, grid_rows - QUAD)
        begin_ref[group] = begin
        fits_ref[group] = (high - begin < QUAD).astype(jnp.int32)
    copies[0].wait()
    for n in range(quads):
        cols = slice(n * QUAD, (n + 1) * QUAD)
        qs[:, cols] = dot(mesh_ref[...], wq_ref[:, cols]).astype(BF16) * BF16(0.125)

    def key_step(t, carry):
        cols = pl.ds(pl.multiple_of(t * QUAD, QUAD), QUAD)
        queries = qs[:, cols]
        head = lax.broadcasted_iota(jnp.int32, queries.shape, 1) // HEAD
        own = jnp.concatenate([jnp.where(head == j, queries, BF16(0)) for j in range(4)], axis=0)
        for n in range(quads):
            some = slice(n * QUAD, (n + 1) * QUAD)
            part = dot_t(own, wkv_ref[some, cols]).astype(BF16)
            pool[pl.ds(t * 4, 4), :, some] = part.reshape(4, mesh_rows, QUAD)
        return carry

    copies[1].wait()
    lax.fori_loop(0, quads, key_step, 0, unroll=4)
    copies[2].wait()
    for side, group in enumerate((0, groups - 1)):
        rows = slice(group * RIM, (group + 1) * RIM)
        qrim_ref[side] = pool[:, rows, :].reshape(heads * RIM, width)
        pooled[:, rows, :] = jnp.zeros((heads, RIM, width), BF16)

    def rows_of(group):
        return pl.ds(pl.multiple_of(group * RIM, RIM), RIM)

    def queries_of(group):
        return pool[:, rows_of(group), :].reshape(heads * RIM, width)

    def put(group, part):
        pooled[:, rows_of(group), :] = part.reshape(heads, RIM, width)

    def group_step(i, carry):
        for k in range(2):
            group = 1 + 2 * i + k
            begin = pl.multiple_of(begin_ref[group], 16)
            rows = x_ref[pl.ds(begin, QUAD), :]
            count = count_edges(rel_ref[rows_of(group), :], begin, QUAD)
            weights = row_weights(queries_of(group), rows, count)
            put(group, dot(weights, rows).astype(BF16))
        return carry

    lax.fori_loop(0, (groups - 2) // 2, group_step, 0, unroll=7)

    def check_step(group, carry):
        @pl.when(fits_ref[group] == 0)
        def _():
            rel = rel_ref[rows_of(group), :]
            put(group, attend_all(queries_of(group), rel, x_ref, total_ref))

        return carry

    lax.fori_loop(1, groups - 1, check_step, 0)

    def value_step(t, carry):
        project_heads(pooled[pl.ds(t * 4, 4)], wkv_ref.at[:, width:], gathered, t)
        return carry

    copies[3].wait()
    lax.fori_loop(0, quads, value_step, 0, unroll=4)
    copies[4].wait()
    for n in range(quads):
        cols = slice(n * QUAD, (n + 1) * QUAD)
        total = mesh_ref[:, cols].astype(F32) + dot(gathered[...], we_ref[:, cols])
        mid_ref[:, cols] = total.astype(BF16)
    norm_ref[...] = layer_norm(mid_ref[...], gain_ref[...])


def rim_kernel(
    rel_ref, shift_ref, low_ref, high_ref, x_hbm, qrim_ref, mesh_ref, wkv_hbm, we_hbm,
    gain_ref, mid_in, norm_in,
    mid_ref, ac_ref, b_ref,
    held_low, held_high, wv_ref, we_ref, pool, gathered, total_ref, sems,
):
    mesh_rows, width = mid_ref.shape
    get_wv = pltpu.make_async_copy(wkv_hbm.at[:, pl.ds(width, width)], wv_ref, sems.at[2])
    get_we = pltpu.make_async_copy(we_hbm, we_ref, sems.at[3])
    grid_rows = x_hbm.shape[0]
    heads = pool.shape[0]
    quads = width // QUAD
    wide = REACH + WIN
    tail = grid_rows - WIN
    near_low = pltpu.make_async_copy(
        x_hbm.at[pl.ds(0, WIN)], held_low.at[pl.ds(REACH, WIN)], sems.at[0]
    )
    near_low.start()
    near_high = pltpu.make_async_copy(
        x_hbm.at[pl.ds(tail, WIN)], held_high.at[pl.ds(tail, WIN)], sems.at[1]
    )
    near_high.start()
    get_wv.start()
    get_we.start()
    held_low[:REACH] = low_ref[...]
    held_high[grid_rows:] = high_ref[...]
    rel_low = rel_ref[:RIM] + REACH
    rel_high = rel_ref[mesh_rows - RIM :]
    count_low = count_edges(rel_low, 0, wide)
    count_high = count_edges(rel_high, tail, wide)
    fits = jnp.max(rel_low.astype(F32)) < wide
    fits_high = jnp.min(rel_high.astype(F32)) >= tail
    near_low.wait()
    near_high.wait()

    def put(side, part):
        pool[:, side * RIM : (side + 1) * RIM, :] = part.reshape(heads, RIM, width)

    weights_low = row_weights(qrim_ref[0], held_low[:wide], count_low)
    weights_high = row_weights(qrim_ref[1], held_high[tail:], count_high)
    put(0, dot(weights_low, held_low[:wide]).astype(BF16))
    put(1, dot(weights_high, held_high[tail:]).astype(BF16))

    @pl.when(jnp.logical_not(jnp.logical_and(fits, fits_high)))
    def _():
        whole_low = pltpu.make_async_copy(x_hbm, held_low.at[pl.ds(REACH, grid_rows)], sems.at[0])
        whole_high = pltpu.make_async_copy(x_hbm, held_high.at[pl.ds(0, grid_rows)], sems.at[1])
        whole_low.start()
        whole_high.start()
        whole_low.wait()
        whole_high.wait()
        put(0, attend_all(qrim_ref[0], rel_low, held_low, total_ref))
        put(1, attend_all(qrim_ref[1], rel_high, held_high, total_ref))

    get_wv.wait()
    for t in range(quads):
        project_heads(pool[t * 4 : (t + 1) * 4], wv_ref, gathered, t)
    get_we.wait()
    edge_mesh = jnp.concatenate([mesh_ref[:RIM], mesh_ref[mesh_rows - RIM :]], axis=0)
    rim_mid = (edge_mesh.astype(F32) + dot(gathered[...], we_ref[...])).astype(BF16)
    rim_norm = layer_norm(rim_mid, gain_ref[...])
    mid_ref[RIM : mesh_rows - RIM] = mid_in[RIM : mesh_rows - RIM]
    mid_ref[:RIM] = rim_mid[:RIM]
    mid_ref[mesh_rows - RIM :] = rim_mid[RIM:]
    tile0 = jnp.concatenate([rim_norm[:RIM], norm_in[RIM:WIN]], axis=0)
    tile1 = jnp.concatenate([norm_in[WIN : mesh_rows - RIM], rim_norm[RIM:]], axis=0)
    first = lax.broadcasted_iota(jnp.int32, tile0.shape, 0) < shift_ref[0]
    ac_ref[...] = jnp.where(first, tile0, tile1)
    b_ref[...] = jnp.where(first, tile1, tile0)


def soft_rows(scores):
    top = jnp.max(scores, axis=-1, keepdims=True)
    grown = jnp.exp(scores - top)
    return (grown / jnp.sum(grown, axis=-1, keepdims=True)).astype(BF16)


def pair_queries(queries):
    second = lax.broadcasted_iota(jnp.int32, queries.shape, 1) >= HEAD
    zero = BF16(0)
    return jnp.concatenate(
        [jnp.where(second, zero, queries), jnp.where(second, queries, zero)], axis=0
    )


def pair_scale(scale_ref, pair, shape):
    upper = lax.broadcasted_iota(jnp.int32, shape, 0) >= shape[0] // 2
    return jnp.where(upper, scale_ref[2 * pair + 1], scale_ref[2 * pair]) * 0.125


def join_pair(wide):
    rows = wide.shape[0] // 2
    second = lax.broadcasted_iota(jnp.int32, (rows, wide.shape[1]), 1) >= HEAD
    return jnp.where(second, wide[rows:], wide[:rows]).astype(BF16)


def inner_kernel(scale_ref, ac_ref, b_ref, w_ref, ac_out, out_ref, qkv):
    width = ac_ref.shape[1]
    rows = jnp.concatenate([ac_ref[...], b_ref[...]], axis=0)
    for n in range(width // QUAD):
        some = slice(n * QUAD, (n + 1) * QUAD)
        for c in range(3):
            at = c * width + n * QUAD
            part = dot(rows, w_ref[:, at : at + QUAD]).astype(BF16)
            ac_out[c, :, some] = part[:WIN]
            qkv[c, :, some] = part[WIN:]
        for pair in range(n * QUAD // LANES, (n + 1) * QUAD // LANES):
            cols = slice(pair * LANES, (pair + 1) * LANES)
            scores = dot_t(pair_queries(qkv[0, :, cols]), qkv[1, :, cols])
            probs = soft_rows(scores * pair_scale(scale_ref, pair, scores.shape))
            out_ref[:, cols] = join_pair(dot(probs, qkv[2, :, cols]))


def cross_kernel(
    scale_ref, shift_ref, low_ref, high_ref, ac_ref, inner_ref, mid_ref, w_ref, wo_ref,
    mixed_ref, keys, values, out0,
):
    width = mid_ref.shape[1]
    shift = shift_ref[0]
    first = lax.broadcasted_iota(jnp.int32, (WIN, width), 0) < shift
    halo = jnp.where(first, high_ref[...], low_ref[...])
    upper = lax.broadcasted_iota(jnp.int32, (WIN, QUAD), 0) < shift
    early = lax.broadcasted_iota(jnp.int32, (2 * WIN, WIN), 0) % WIN < shift
    zero = BF16(0)
    for n in range(width // QUAD):
        some = slice(n * QUAD, (n + 1) * QUAD)
        for c, held in enumerate((keys, values)):
            at = (c + 1) * width + n * QUAD
            part = dot(halo, w_ref[:, at : at + QUAD]).astype(BF16)
            own = ac_ref[c + 1, :, some]
            held[:WIN, some] = jnp.where(upper, own, part)
            held[WIN:, some] = jnp.where(upper, part, own)
        for pair in range(n * QUAD // LANES, (n + 1) * QUAD // LANES):
            cols = slice(pair * LANES, (pair + 1) * LANES)
            both = dot_t(pair_queries(ac_ref[0, :, cols]), keys[:, cols])
            scores = jnp.where(early, both[:, :WIN], both[:, WIN:])
            probs = soft_rows(scores * pair_scale(scale_ref, pair, scores.shape))
            wide = jnp.concatenate(
                [jnp.where(early, probs, zero), jnp.where(early, zero, probs)], axis=1
            )
            part = join_pair(dot(wide, values[:, cols]))
            inner = inner_ref[:, cols]
            out0[:WIN, cols] = jnp.where(early[:WIN], part, inner)
            out0[WIN:, cols] = jnp.where(early[:WIN], inner, part)
    for n in range(width // QUAD):
        some = slice(n * QUAD, (n + 1) * QUAD)
        total = mid_ref[:, some].astype(F32) + dot(out0[...], wo_ref[:, some])
        mixed_ref[:, some] = total.astype(BF16)


VMEM = pl.BlockSpec(memory_space=pltpu.VMEM)
SMEM = pl.BlockSpec(memory_space=pltpu.SMEM)
ANY = pl.BlockSpec(memory_space=pl.ANY)
HBM = pl.BlockSpec(memory_space=pltpu.HBM)


def call(kernel, out_shape, in_specs, scratch, mib, flops, moved, name):
    return pl.pallas_call(
        kernel,
        out_shape=out_shape,
        in_specs=in_specs,
        out_specs=jax.tree.map(lambda _: VMEM, out_shape),
        scratch_shapes=scratch,
        compiler_params=pltpu.CompilerParams(vmem_limit_bytes=mib * 2**20),
        cost_estimate=pl.CostEstimate(flops=flops, bytes_accessed=moved, transcendentals=0),
        name=name,
    )


def local(
    grid_features,
    mesh_features,
    sources,
    window_shift,
    w_query,
    w_grid_kv,
    w_enc_out,
    norm_gain,
    w_win_qkv,
    w_win_out,
    head_scale,
):
    grid_rows, width = grid_features.shape
    mesh_rows = mesh_features.shape[0]
    heads = head_scale.shape[0]
    bands = lax.axis_size("band")
    forward = [(i, i + 1) for i in range(bands - 1)]
    backward = [(b, a) for a, b in forward]
    strip = jax.ShapeDtypeStruct((REACH, width), BF16)
    first_rows, last_rows = call(
        halo_kernel, (strip, strip), [VMEM, VMEM], [], 8, HALO_FLOPS, HALO_BYTES, "halo",
    )(grid_features[:REACH], grid_features[grid_rows - REACH :])
    low = lax.ppermute(last_rows, "band", forward)
    high = lax.ppermute(first_rows, "band", backward)
    rel = sources - lax.axis_index("band") * grid_rows
    gain = norm_gain.reshape(1, width)

    def arr(*shape, dtype=BF16):
        return jax.ShapeDtypeStruct(shape, dtype)

    full = (mesh_rows, width)
    tile = (WIN, width)
    spread = pltpu.VMEM((heads, mesh_rows, width), BF16)
    total = pltpu.VMEM((heads * RIM, width), F32)
    groups = mesh_rows // RIM
    mid, norm, qrim = call(
        interior_kernel,
        (arr(*full), arr(*full), arr(2, heads * RIM, width)),
        [VMEM, HBM, VMEM, HBM, HBM, HBM, VMEM],
        [
            pltpu.VMEM((grid_rows, width), BF16),
            pltpu.VMEM((width, width), BF16),
            pltpu.VMEM((width, 2 * width), BF16),
            pltpu.VMEM((width, width), BF16),
            spread, spread,
            pltpu.VMEM(full, BF16),
            pltpu.VMEM(full, BF16),
            total,
            pltpu.SMEM((groups,), jnp.int32),
            pltpu.SMEM((groups,), jnp.int32),
            pltpu.SemaphoreType.DMA((5,)),
        ],
        52, 10**10, 3 * 10**7, "interior",
    )(rel, grid_features, mesh_features, w_query, w_grid_kv, w_enc_out, gain)

    held = pltpu.VMEM((grid_rows + REACH, width), BF16)
    mid, ac, b = call(
        rim_kernel,
        (arr(*full), arr(*tile), arr(*tile)),
        [VMEM, SMEM, VMEM, VMEM, HBM, VMEM, VMEM, HBM, HBM, VMEM, VMEM, VMEM],
        [
            held, held,
            pltpu.VMEM((width, width), BF16),
            pltpu.VMEM((width, width), BF16),
            pltpu.VMEM((heads, 2 * RIM, width), BF16),
            pltpu.VMEM((2 * RIM, width), BF16),
            total,
            pltpu.SemaphoreType.DMA((4,)),
        ],
        52, 10**9, 10**7, "rims",
    )(
        rel, window_shift, low, high, grid_features, qrim, mesh_features, w_grid_kv, w_enc_out,
        gain, mid, norm,
    )

    around = forward + [(bands - 1, 0)]
    low_norm = lax.ppermute(ac, "band", around)
    high_norm = lax.ppermute(ac, "band", [(b_, a_) for a_, b_ in around])

    qkv_ac, inner = call(
        inner_kernel,
        (arr(3, *tile), arr(*tile)),
        [SMEM, VMEM, VMEM, VMEM],
        [pltpu.VMEM((3, *tile), BF16)],
        16, 2 * 10**9, 10**7, "inner",
    )(head_scale, ac, b, w_win_qkv)

    return call(
        cross_kernel,
        arr(*full),
        [SMEM, SMEM, VMEM, VMEM, VMEM, VMEM, VMEM, VMEM, VMEM],
        [
            pltpu.VMEM((2 * WIN, width), BF16),
            pltpu.VMEM((2 * WIN, width), BF16),
            pltpu.VMEM(full, BF16),
        ],
        16, 2 * 10**9, 10**7, "cross",
    )(head_scale, window_shift, low_norm, high_norm, qkv_ac, inner, mid, w_win_qkv, w_win_out)


def solution(mesh):
    placed = (P("band", None),) * 3 + (P(),) * 8
    return jax.shard_map(
        local, mesh=mesh, in_specs=placed, out_specs=P("band", None), check_vma=False
    )
```

profile of v0, /device:TPU:0, one launch (start us, length us, event | category | flops | bytes accessed | tf_op | source)
XLA Modules:
  0.0 51.0 jit_solution(14869299200308080427)
XLA Ops:
  0.0 1.5 %fusion = (bf16[384,1024]{1,0:T(8,128)(2,1)S(1)}, bf16[384,1024]{1,0:T(8,128)(2,1)S(1)}) fusion(bf16[3072,1024]{1,0:T(8,128)(2,1)} %x_hbm.3), kind=kLoop, calls=%fused_computation.1 | loop fusion | bytes 3145728 | tf_op jit(solution)/shard_map/slice | solution.py:402
  1.5 0.0 copy-start.1
  1.5 0.0 copy-start.4
  1.5 0.0 slice-start
  1.5 1.0 %halo.1 = (bf16[384,1024]{1,0:T(8,128)(2,1)S(1)}, bf16[384,1024]{1,0:T(8,128)(2,1)}) custom-call(bf16[384,1024]{1,0:T(8,128)(2,1)S(1)} %get-tuple-element.26.first_in, bf16[384,1024]{1,0:T(8,128)(2,1)S(1)} %get-tuple-element.25.last_in), custom_call_target="tpu_custom_call" | custom-call | flops 10000000000 | bytes 30000000 | tf_op jit(solution)/shard_map/halo/pallas_call | solution.py:400
  2.6 3.4 %collective-permute-start = (bf16[384,1024]{1,0:T(8,128)(2,1)}, bf16[384,1024]{1,0:T(8,128)(2,1)}, u32[]{:S(2)}, u32[]{:S(2)}) collective-permute-start(bf16[384,1024]{1,0:T(8,128)(2,1)} %get-tuple-element.15), channel_id=1, source_target_pairs={{0,1},{1,2},{2,3},{3,4},{4,5},{5,6},{6,7},{7,8},{8,9},{9,10},{10,1... | collective-permute-start | bytes 2359304 | tf_op jit(solution)/shard_map/ppermute | solution.py:403
  5.9 1.3 %collective-permute-start.1 = (bf16[384,1024]{1,0:T(8,128)(2,1)S(1)}, bf16[384,1024]{1,0:T(8,128)(2,1)}, u32[]{:S(2)}, u32[]{:S(2)}) collective-permute-start(bf16[384,1024]{1,0:T(8,128)(2,1)S(1)} %get-tuple-element.16), channel_id=1, source_target_pairs={{1,0},{2,1},{3,2},{4,3},{5,4},{6,5},{7,6},{8,7},{9,8},{10,9},{11,1... | collective-permute-start | bytes 2359304 | tf_op jit(solution)/shard_map/ppermute | solution.py:404
  7.9 0.8 %copy.12 = s32[256,12]{1,0:T(8,128)S(1)} copy(s32[256,12]{0,1:T(8,128)} %param.13) | data formatting | bytes 24576 | tf_op args[2]
  8.8 0.0 slice-start.1
  8.8 14.2 %interior.1 = (bf16[256,1024]{1,0:T(8,128)(2,1)S(1)}, bf16[256,1024]{1,0:T(8,128)(2,1)S(1)}, bf16[2,256,1024]{2,1,0:T(8,128)(2,1)}) custom-call(s32[256,12]{1,0:T(8,128)S(1)} %broadcast_subtract_fusion.rel_ref, bf16[3072,1024]{1,0:T(8,128)(2,1)} %x_hbm.3, bf16[256,1024]{1,0:T(8,128)(2,1)S(1)} %copy-done.1, bf16[1024,1024]{1,0:T(8,128)(2,1)} %wq_hbm.1, ...), custom_call_target="tpu_custom_call" | custom-call | flops 10000000000 | bytes 30000000 | tf_op jit(solution)/shard_map/interior/pallas_call | solution.py:416
  23.0 0.0 copy-start.2
  23.0 0.8 %copy-done.2 = bf16[256,1024]{1,0:T(8,128)(2,1)} copy-done((bf16[256,1024]{1,0:T(8,128)(2,1)}, bf16[256,1024]{1,0:T(8,128)(2,1)S(1)}, u32[]{:S(2)}) %copy-start.2) | copy-done | bytes 524312
  23.8 0.8 %copy-done.3 = bf16[256,1024]{1,0:T(8,128)(2,1)} copy-done((bf16[256,1024]{1,0:T(8,128)(2,1)}, bf16[256,1024]{1,0:T(8,128)(2,1)S(1)}, u32[]{:S(2)}) %copy-start.3) | copy-done | bytes 524312
  24.5 0.0 collective-permute-done.low_ref
  24.6 0.0 collective-permute-done.1.high_ref
  24.6 5.5 %rims.1 = (bf16[256,1024]{1,0:T(8,128)(2,1)S(1)}, bf16[128,1024]{1,0:T(8,128)(2,1)S(1)}, bf16[128,1024]{1,0:T(8,128)(2,1)S(1)}) custom-call(s32[256,12]{1,0:T(8,128)S(1)} %broadcast_subtract_fusion.rel_ref, s32[1]{0:T(128)S(6)} %copy.13.shift_ref, bf16[384,1024]{1,0:T(8,128)(2,1)} %collective-permute-done.low_ref, ...), custom_call_target="tpu_custom_call" | custom-call | flops 1000000000 | bytes 10000000 | tf_op jit(solution)/shard_map/rims/pallas_call | solution.py:437
  30.1 0.0 copy-start
  30.1 7.3 %collective-permute-start.3 = (bf16[128,1024]{1,0:T(8,128)(2,1)S(1)}, bf16[128,1024]{1,0:T(8,128)(2,1)S(1)}, u32[]{:S(2)}, u32[]{:S(2)}) collective-permute-start(bf16[128,1024]{1,0:T(8,128)(2,1)S(1)} %get-tuple-element.20.ac_ref), channel_id=1, source_target_pairs={{1,0},{2,1},{3,2},{4,3},{5,4},{6,5},{7,6},{8,7},{9,8},{10,9},{11,1... | collective-permute-start | bytes 786440 | tf_op jit(solution)/shard_map/ppermute | solution.py:458
  37.4 0.0 collective-permute-start.2
  37.4 0.0 copy-done.5
  37.4 5.0 %inner.1 = (bf16[3,128,1024]{2,1,0:T(8,128)(2,1)S(1)}, bf16[128,1024]{1,0:T(8,128)(2,1)S(1)}) custom-call(f32[16]{0:T(128)S(1)} %copy-done.5, bf16[128,1024]{1,0:T(8,128)(2,1)S(1)} %get-tuple-element.20.ac_ref, bf16[128,1024]{1,0:T(8,128)(2,1)S(1)} %get-tuple-element.21.b_ref, bf16[1024,3072]{1,0:T(8,128)(2,1)S(1)} %bitcast.2), custom_call_target="tpu_custom_call" | custom-call | flops 2000000000 | bytes 10000000 | tf_op jit(solution)/shard_map/inner/pallas_call | solution.py:460
  42.4 0.0 collective-permute-done.3.high_ref
  42.4 4.4 %collective-permute-done.2.low_ref = bf16[128,1024]{1,0:T(8,128)(2,1)S(1)} collective-permute-done((bf16[128,1024]{1,0:T(8,128)(2,1)S(1)}, bf16[128,1024]{1,0:T(8,128)(2,1)S(1)}, u32[]{:S(2)}, u32[]{:S(2)}) %collective-permute-start.2) | collective-permute-done | bytes 262176 | tf_op jit(solution)/shard_map/ppermute | solution.py:457
  46.8 4.2 %cross.1 = bf16[256,1024]{1,0:T(8,128)(2,1)} custom-call(f32[16]{0:T(128)S(1)} %copy-done.5, s32[1]{0:T(128)S(6)} %copy.13.shift_ref, bf16[128,1024]{1,0:T(8,128)(2,1)S(1)} %collective-permute-done.2.low_ref, bf16[128,1024]{1,0:T(8,128)(2,1)S(1)} %collective-permute-done.3.high_ref, bf16[3,128,1024]{2,1,0:T(8,128)(2,1)S(1)} %get-tuple-element.22.ac_ref, ...), custom_call_target="tpu_custom_call" | custom-call | flops 2000000000 | bytes 10000000 | tf_op jit(solution)/shard_map/cross/pallas_call | solution.py:468
  (9 shorter events, 0.0 us)
Async XLA Ops:
  1.5 7.2 %copy-start.1 = (bf16[256,1024]{1,0:T(8,128)(2,1)S(1)}, bf16[256,1024]{1,0:T(8,128)(2,1)}, u32[]{:S(2)}) copy-start(bf16[256,1024]{1,0:T(8,128)(2,1)} %mesh_ref.3) | copy-start | bytes 1572868
  1.5 7.2 %copy-start.4 = (f32[1024]{0:T(1024)S(1)}, f32[1024]{0:T(1024)}, u32[]{:S(2)}) copy-start(f32[1024]{0:T(1024)} %param.18) | copy-start | bytes 12292
  1.5 35.9 %slice-start = ((s8[6291456]{0:T(1024)(128)(4,1)}), s8[2097152]{0:T(1024)(128)(4,1)S(1)}, s32[]{:S(2)}) async-start(s8[6291456]{0:T(1024)(128)(4,1)} %bitcast.1), calls=%async_computation | async-start | bytes 4194304
  2.6 22.0 %collective-permute-start = (bf16[384,1024]{1,0:T(8,128)(2,1)}, bf16[384,1024]{1,0:T(8,128)(2,1)}, u32[]{:S(2)}, u32[]{:S(2)}) collective-permute-start(bf16[384,1024]{1,0:T(8,128)(2,1)} %get-tuple-element.15), channel_id=1, source_target_pairs={{0,1},{1,2},{2,3},{3,4},{4,5},{5,6},{6,7},{7,8},{8,9},{9,10},{10,1... | collective-permute-start | bytes 2359304 | tf_op jit(solution)/shard_map/ppermute | solution.py:403
  5.9 18.6 %collective-permute-start.1 = (bf16[384,1024]{1,0:T(8,128)(2,1)S(1)}, bf16[384,1024]{1,0:T(8,128)(2,1)}, u32[]{:S(2)}, u32[]{:S(2)}) collective-permute-start(bf16[384,1024]{1,0:T(8,128)(2,1)S(1)} %get-tuple-element.16), channel_id=1, source_target_pairs={{1,0},{2,1},{3,2},{4,3},{5,4},{6,5},{7,6},{8,7},{9,8},{10,9},{11,1... | collective-permute-start | bytes 2359304 | tf_op jit(solution)/shard_map/ppermute | solution.py:404
  8.8 28.6 %slice-start.1 = ((s8[6291456]{0:T(1024)(128)(4,1)}), s8[4194304]{0:T(1024)(128)(4,1)S(1)}, s32[]{:S(2)}) async-start(s8[6291456]{0:T(1024)(128)(4,1)} %bitcast.1), calls=%async_computation.1 | async-start | bytes 8388608
  23.0 0.8 %copy-start.2 = (bf16[256,1024]{1,0:T(8,128)(2,1)}, bf16[256,1024]{1,0:T(8,128)(2,1)S(1)}, u32[]{:S(2)}) copy-start(bf16[256,1024]{1,0:T(8,128)(2,1)S(1)} %get-tuple-element.18.mid_in) | copy-start | bytes 1572868
  23.7 0.8 %copy-start.3 = (bf16[256,1024]{1,0:T(8,128)(2,1)}, bf16[256,1024]{1,0:T(8,128)(2,1)S(1)}, u32[]{:S(2)}) copy-start(bf16[256,1024]{1,0:T(8,128)(2,1)S(1)} %get-tuple-element.19.norm_in) | copy-start | bytes 1572868
  24.6 12.8 %copy-start.5 = (f32[16]{0:T(128)S(1)}, f32[16]{0:T(128)}, u32[]{:S(2)}) copy-start(f32[16]{0:T(128)} %scale_ref.3) | copy-start | bytes 196
  30.1 16.7 %copy-start = (bf16[1024,1024]{1,0:T(8,128)(2,1)S(1)}, bf16[1024,1024]{1,0:T(8,128)(2,1)}, u32[]{:S(2)}) copy-start(bf16[1024,1024]{1,0:T(8,128)(2,1)} %wo_ref.1) | copy-start | bytes 6291460
  30.1 12.3 %collective-permute-start.3 = (bf16[128,1024]{1,0:T(8,128)(2,1)S(1)}, bf16[128,1024]{1,0:T(8,128)(2,1)S(1)}, u32[]{:S(2)}, u32[]{:S(2)}) collective-permute-start(bf16[128,1024]{1,0:T(8,128)(2,1)S(1)} %get-tuple-element.20.ac_ref), channel_id=1, source_target_pairs={{1,0},{2,1},{3,2},{4,3},{5,4},{6,5},{7,6},{8,7},{9,8},{10,9},{11,1... | collective-permute-start | bytes 786440 | tf_op jit(solution)/shard_map/ppermute | solution.py:458
  37.4 9.4 %collective-permute-start.2 = (bf16[128,1024]{1,0:T(8,128)(2,1)S(1)}, bf16[128,1024]{1,0:T(8,128)(2,1)S(1)}, u32[]{:S(2)}, u32[]{:S(2)}) collective-permute-start(bf16[128,1024]{1,0:T(8,128)(2,1)S(1)} %get-tuple-element.20.ac_ref), channel_id=1, source_target_pairs={{0,1},{1,2},{2,3},{3,4},{4,5},{5,6},{6,7},{7,8},{8,9},{9,10},{10,1... | collective-permute-start | bytes 786440 | tf_op jit(solution)/shard_map/ppermute | solution.py:457
where the time goes:
time: 51.3 us; the launch traced here: 51 us
  Pallas kernels  29.9 us (58%)
  starting transfers between devices  11.9 us (23%)
  waiting for transfers between devices  4.38 us (9%)
  local copies, waits for them, and re-layouts  3.94 us (8%)
  between operations  0.8 us (2%)
    pallas_call x1, Pallas kernels, local(): call(interior_kernel, (arr(*full), arr(*full), arr(2, heads * RIM, width)...  14.2 us
    ppermute x1, starting transfers between devices, local(): high_norm = lax.ppermute(ac, 'band', [(b_, a_) for a_, b_ in around])  7.26 us
    pallas_call x1, Pallas kernels, local(): call(rim_kernel, (arr(*full), arr(*tile), arr(*tile)), [VMEM, SMEM, VMEM,...  5.54 us
    pallas_call x1, Pallas kernels, local(): call(inner_kernel, (arr(3, *tile), arr(*tile)), [SMEM, VMEM, VMEM, VMEM],...  4.97 us
    ppermute x1, waiting for transfers between devices, local(): low_norm = lax.ppermute(ac, 'band', around)  4.37 us
    pallas_call x1, Pallas kernels, local(): call(cross_kernel, arr(*full), [SMEM, SMEM, VMEM, VMEM, VMEM, VMEM, VMEM,...  4.2 us
    ppermute x1, starting transfers between devices, local(): low = lax.ppermute(last_rows, 'band', forward)  3.39 us
    unnamed x17, local copies, waits for them, and re-layouts  2.45 us
  transfers between devices with their start and end apart: 4, of which 1 were waited for; matrix products, arithmetic and copies ran while one was open for 2% of the time, Pallas kernels for 38%

commit v1 on v0

--- a/solution.py
+++ b/solution.py
@@ -1,3 +1,5 @@
+import functools
+
 import jax
 import jax.numpy as jnp
 from jax import lax
@@ -36,7 +38,7 @@
 
 def count_edges(rel, start, cols):
     nodes, edge_count = rel.shape
-    row = lax.broadcasted_iota(jnp.int32, (nodes, cols), 1) + start
+    row = (lax.broadcasted_iota(jnp.int32, (nodes, cols), 1) + start).astype(F32)
     total = jnp.zeros((nodes, cols), F32)
     for e in range(edge_count):
         total += (rel[:, e : e + 1] == row).astype(F32)
@@ -101,16 +103,28 @@
     out_ref[:, cols] = total.astype(BF16)
 
 
-def halo_kernel(first_in, last_in, first_ref, last_ref):
-    first_ref[...] = first_in[...]
-    last_ref[...] = last_in[...]
+def halo_kernel(side_ref, x_hbm, near_ref, far_ref, sems):
+    rows = near_ref.shape[0]
+    tail = x_hbm.shape[0] - rows
+    near_at = jnp.where(side_ref[0] == 0, tail, 0)
+    copies = []
+    for i, (at, target) in enumerate(((tail - near_at, far_ref), (near_at, near_ref))):
+        for k in range(rows // WIN):
+            place = pl.ds(pl.multiple_of(at + k * WIN, WIN), WIN)
+            sem = sems.at[i * (rows // WIN) + k]
+            target_rows = target.at[pl.ds(k * WIN, WIN)]
+            copies.append(pltpu.make_async_copy(x_hbm.at[place], target_rows, sem))
+    for copy in copies:
+        copy.start()
+    for copy in copies:
+        copy.wait()
 
 
 def interior_kernel(
-    rel_ref, x_hbm, mesh_ref, wq_hbm, wkv_hbm, we_hbm, gain_ref,
-    mid_ref, norm_ref, qrim_ref,
+    edge_count, shift_ref, edge_ref, x_hbm, mesh_ref, wq_hbm, wkv_hbm, we_hbm, gain_ref,
+    mid_ref, ac_ref, b_ref, qrim_ref,
     x_ref, wq_ref, wkv_ref, we_ref,
-    pool, pooled, qs, gathered, total_ref, begin_ref, fits_ref, sems,
+    rel_ref, pool, pooled, qs, gathered, total_ref, begin_ref, fits_ref, sems,
 ):
     width = mesh_ref.shape[1]
     key_cols, value_cols = pl.ds(0, width), pl.ds(width, width)
@@ -132,8 +146,9 @@
     grid_rows = x_ref.shape[0]
     quads = width // QUAD
     groups = mesh_rows // RIM
+    rel_ref[...] = edge_ref[...].astype(F32).T
     for group in range(1, groups - 1):
-        rel = rel_ref[group * RIM : (group + 1) * RIM, :].astype(F32)
+        rel = rel_ref[group * RIM : (group + 1) * RIM, :edge_count]
         low = jnp.min(rel).astype(jnp.int32)
         high = jnp.max(rel).astype(jnp.int32)
         begin = jnp.clip(low // 16 * 16, 0, grid_rows - QUAD)
@@ -177,7 +192,7 @@
             group = 1 + 2 * i + k
             begin = pl.multiple_of(begin_ref[group], 16)
             rows = x_ref[pl.ds(begin, QUAD), :]
-            count = count_edges(rel_ref[rows_of(group), :], begin, QUAD)
+            count = count_edges(rel_ref[rows_of(group), :edge_count], begin, QUAD)
             weights = row_weights(queries_of(group), rows, count)
             put(group, dot(weights, rows).astype(BF16))
         return carry
@@ -187,7 +202,7 @@
     def check_step(group, carry):
         @pl.when(fits_ref[group] == 0)
         def _():
-            rel = rel_ref[rows_of(group), :]
+            rel = rel_ref[rows_of(group), :edge_count]
             put(group, attend_all(queries_of(group), rel, x_ref, total_ref))
 
         return carry
@@ -205,12 +220,15 @@
         cols = slice(n * QUAD, (n + 1) * QUAD)
         total = mesh_ref[:, cols].astype(F32) + dot(gathered[...], we_ref[:, cols])
         mid_ref[:, cols] = total.astype(BF16)
-    norm_ref[...] = layer_norm(mid_ref[...], gain_ref[...])
+    norm = layer_norm(mid_ref[...], gain_ref[...])
+    first = lax.broadcasted_iota(jnp.int32, (WIN, width), 0) < shift_ref[0]
+    ac_ref[...] = jnp.where(first, norm[:WIN], norm[WIN:])
+    b_ref[...] = jnp.where(first, norm[WIN:], norm[:WIN])
 
 
 def rim_kernel(
-    rel_ref, shift_ref, low_ref, high_ref, x_hbm, qrim_ref, mesh_ref, wkv_hbm, we_hbm,
-    gain_ref, mid_in, norm_in,
+    edge_count, side_ref, shift_ref, edge_ref, near_ref, far_ref, x_hbm, qrim_ref, mesh_ref, wkv_hbm, we_hbm,
+    gain_ref, mid_in, ac_in, b_in,
     mid_ref, ac_ref, b_ref,
     held_low, held_high, wv_ref, we_ref, pool, gathered, total_ref, sems,
 ):
@@ -232,14 +250,25 @@
     near_high.start()
     get_wv.start()
     get_we.start()
-    held_low[:REACH] = low_ref[...]
-    held_high[grid_rows:] = high_ref[...]
-    rel_low = rel_ref[:RIM] + REACH
-    rel_high = rel_ref[mesh_rows - RIM :]
+    even = side_ref[0] == 0
+
+    @pl.when(even)
+    def _():
+        held_low[:REACH] = far_ref[...]
+        held_high[grid_rows:] = near_ref[...]
+
+    @pl.when(jnp.logical_not(even))
+    def _():
+        held_low[:REACH] = near_ref[...]
+        held_high[grid_rows:] = far_ref[...]
+
+    rel = edge_ref[...].astype(F32).T
+    rel_low = rel[:RIM, :edge_count] + float(REACH)
+    rel_high = rel[mesh_rows - RIM :, :edge_count]
     count_low = count_edges(rel_low, 0, wide)
     count_high = count_edges(rel_high, tail, wide)
-    fits = jnp.max(rel_low.astype(F32)) < wide
-    fits_high = jnp.min(rel_high.astype(F32)) >= tail
+    fits = jnp.max(rel_low) < wide
+    fits_high = jnp.min(rel_high) >= tail
     near_low.wait()
     near_high.wait()
 
@@ -269,14 +298,15 @@
     edge_mesh = jnp.concatenate([mesh_ref[:RIM], mesh_ref[mesh_rows - RIM :]], axis=0)
     rim_mid = (edge_mesh.astype(F32) + dot(gathered[...], we_ref[...])).astype(BF16)
     rim_norm = layer_norm(rim_mid, gain_ref[...])
-    mid_ref[RIM : mesh_rows - RIM] = mid_in[RIM : mesh_rows - RIM]
-    mid_ref[:RIM] = rim_mid[:RIM]
-    mid_ref[mesh_rows - RIM :] = rim_mid[RIM:]
-    tile0 = jnp.concatenate([rim_norm[:RIM], norm_in[RIM:WIN]], axis=0)
-    tile1 = jnp.concatenate([norm_in[WIN : mesh_rows - RIM], rim_norm[RIM:]], axis=0)
-    first = lax.broadcasted_iota(jnp.int32, tile0.shape, 0) < shift_ref[0]
-    ac_ref[...] = jnp.where(first, tile0, tile1)
-    b_ref[...] = jnp.where(first, tile1, tile0)
+    row = lax.broadcasted_iota(jnp.int32, (RIM, width), 0)
+    for side in range(2):
+        part = slice(side * RIM, (side + 1) * RIM)
+        at = slice(side * (mesh_rows - RIM), side * (mesh_rows - RIM) + RIM)
+        mid_ref[at] = rim_mid[part]
+        at = slice(side * (WIN - RIM), side * (WIN - RIM) + RIM)
+        crosses = (row + at.start < shift_ref[0]).astype(jnp.int32) != side
+        ac_ref[at] = jnp.where(crosses, rim_norm[part], ac_in[at])
+        b_ref[at] = jnp.where(crosses, b_in[at], rim_norm[part])
 
 
 def soft_rows(scores):
@@ -322,13 +352,13 @@
 
 
 def cross_kernel(
-    scale_ref, shift_ref, low_ref, high_ref, ac_ref, inner_ref, mid_ref, w_ref, wo_ref,
+    scale_ref, side_ref, shift_ref, near_ref, far_ref, ac_ref, inner_ref, mid_ref, w_ref, wo_ref,
     mixed_ref, keys, values, out0,
 ):
     width = mid_ref.shape[1]
     shift = shift_ref[0]
-    first = lax.broadcasted_iota(jnp.int32, (WIN, width), 0) < shift
-    halo = jnp.where(first, high_ref[...], low_ref[...])
+    first = (lax.broadcasted_iota(jnp.int32, (WIN, width), 0) < shift).astype(jnp.int32)
+    halo = jnp.where(first != side_ref[0], near_ref[...], far_ref[...])
     upper = lax.broadcasted_iota(jnp.int32, (WIN, QUAD), 0) < shift
     early = lax.broadcasted_iota(jnp.int32, (2 * WIN, WIN), 0) % WIN < shift
     zero = BF16(0)
@@ -364,13 +394,14 @@
 HBM = pl.BlockSpec(memory_space=pltpu.HBM)
 
 
-def call(kernel, out_shape, in_specs, scratch, mib, flops, moved, name):
+def call(kernel, out_shape, in_specs, scratch, mib, flops, moved, name, aliases={}):
     return pl.pallas_call(
         kernel,
         out_shape=out_shape,
         in_specs=in_specs,
         out_specs=jax.tree.map(lambda _: VMEM, out_shape),
         scratch_shapes=scratch,
+        input_output_aliases=aliases,
         compiler_params=pltpu.CompilerParams(vmem_limit_bytes=mib * 2**20),
         cost_estimate=pl.CostEstimate(flops=flops, bytes_accessed=moved, transcendentals=0),
         name=name,
@@ -393,16 +424,21 @@
     grid_rows, width = grid_features.shape
     mesh_rows = mesh_features.shape[0]
     heads = head_scale.shape[0]
+    edge_count = sources.shape[1]
     bands = lax.axis_size("band")
-    forward = [(i, i + 1) for i in range(bands - 1)]
-    backward = [(b, a) for a, b in forward]
+    band = lax.axis_index("band")
+    side = (band % 2).astype(jnp.int32).reshape(1)
+    near = [(i, i ^ 1) for i in range(bands)]
+    far = [pair for i in range(1, bands - 1, 2) for pair in ((i, i + 1), (i + 1, i))]
+    around = far + [(bands - 1, 0), (0, bands - 1)]
     strip = jax.ShapeDtypeStruct((REACH, width), BF16)
-    first_rows, last_rows = call(
-        halo_kernel, (strip, strip), [VMEM, VMEM], [], 8, HALO_FLOPS, HALO_BYTES, "halo",
-    )(grid_features[:REACH], grid_features[grid_rows - REACH :])
-    low = lax.ppermute(last_rows, "band", forward)
-    high = lax.ppermute(first_rows, "band", backward)
-    rel = sources - lax.axis_index("band") * grid_rows
+    near_rows, far_rows = call(
+        halo_kernel, (strip, strip), [SMEM, HBM],
+        [pltpu.SemaphoreType.DMA((2 * REACH // WIN,))], 57, HALO_FLOPS, HALO_BYTES, "halo",
+    )(side, grid_features)
+    far_grid = lax.ppermute(far_rows, "band", far)
+    near_grid = lax.ppermute(near_rows, "band", near)
+    rel = jnp.pad(sources.T - band * grid_rows, ((0, -edge_count % 8), (0, 0)))
     gain = norm_gain.reshape(1, width)
 
     def arr(*shape, dtype=BF16):
@@ -413,15 +449,16 @@
     spread = pltpu.VMEM((heads, mesh_rows, width), BF16)
     total = pltpu.VMEM((heads * RIM, width), F32)
     groups = mesh_rows // RIM
-    mid, norm, qrim = call(
-        interior_kernel,
-        (arr(*full), arr(*full), arr(2, heads * RIM, width)),
-        [VMEM, HBM, VMEM, HBM, HBM, HBM, VMEM],
+    mid, ac, b, qrim = call(
+        functools.partial(interior_kernel, edge_count),
+        (arr(*full), arr(*tile), arr(*tile), arr(2, heads * RIM, width)),
+        [SMEM, VMEM, HBM, VMEM, HBM, HBM, HBM, VMEM],
         [
             pltpu.VMEM((grid_rows, width), BF16),
             pltpu.VMEM((width, width), BF16),
             pltpu.VMEM((width, 2 * width), BF16),
             pltpu.VMEM((width, width), BF16),
+            pltpu.VMEM((mesh_rows, rel.shape[0]), F32),
             spread, spread,
             pltpu.VMEM(full, BF16),
             pltpu.VMEM(full, BF16),
@@ -431,13 +468,13 @@
             pltpu.SemaphoreType.DMA((5,)),
         ],
         52, 10**10, 3 * 10**7, "interior",
-    )(rel, grid_features, mesh_features, w_query, w_grid_kv, w_enc_out, gain)
+    )(window_shift, rel, grid_features, mesh_features, w_query, w_grid_kv, w_enc_out, gain)
 
     held = pltpu.VMEM((grid_rows + REACH, width), BF16)
     mid, ac, b = call(
-        rim_kernel,
+        functools.partial(rim_kernel, edge_count),
         (arr(*full), arr(*tile), arr(*tile)),
-        [VMEM, SMEM, VMEM, VMEM, HBM, VMEM, VMEM, HBM, HBM, VMEM, VMEM, VMEM],
+        [SMEM, SMEM, VMEM, VMEM, VMEM, HBM, VMEM, VMEM, HBM, HBM] + [VMEM] * 4,
         [
             held, held,
             pltpu.VMEM((width, width), BF16),
@@ -447,15 +484,14 @@
             total,
             pltpu.SemaphoreType.DMA((4,)),
         ],
-        52, 10**9, 10**7, "rims",
+        50, 10**9, 10**7, "rims", {11: 0, 12: 1, 13: 2},
     )(
-        rel, window_shift, low, high, grid_features, qrim, mesh_features, w_grid_kv, w_enc_out,
-        gain, mid, norm,
+        side, window_shift, rel, near_grid, far_grid, grid_features, qrim, mesh_features,
+        w_grid_kv, w_enc_out, gain, mid, ac, b,
     )
 
-    around = forward + [(bands - 1, 0)]
-    low_norm = lax.ppermute(ac, "band", around)
-    high_norm = lax.ppermute(ac, "band", [(b_, a_) for a_, b_ in around])
+    far_norm = lax.ppermute(ac, "band", around)
+    near_norm = lax.ppermute(ac, "band", near)
 
     qkv_ac, inner = call(
         inner_kernel,
@@ -468,14 +504,14 @@
     return call(
         cross_kernel,
         arr(*full),
-        [SMEM, SMEM, VMEM, VMEM, VMEM, VMEM, VMEM, VMEM, VMEM],
+        [SMEM] * 3 + [VMEM] * 7,
         [
             pltpu.VMEM((2 * WIN, width), BF16),
             pltpu.VMEM((2 * WIN, width), BF16),
             pltpu.VMEM(full, BF16),
         ],
         16, 2 * 10**9, 10**7, "cross",
-    )(head_scale, window_shift, low_norm, high_norm, qkv_ac, inner, mid, w_win_qkv, w_win_out)
+    )(head_scale, side, window_shift, near_norm, far_norm, qkv_ac, inner, mid, w_win_qkv, w_win_out)
 
 
 def solution(mesh):

time: 51.3 us -> 43.3 us (0.84)
  the two profiles are of different devices: /device:TPU:0 before, /device:TPU:11 now
where the time goes in v1:
time: 43.3 us; the launch traced here: 43.2 us
  Pallas kernels  31 us (72%)
  waiting for transfers between devices  6.02 us (14%)
  starting transfers between devices  5.26 us (12%)
  between operations  0.79 us (2%)
    pallas_call x1, Pallas kernels, local(): call(functools.partial(interior_kernel, edge_count), (arr(*full), arr(*ti...  14.2 us
    pallas_call x1, Pallas kernels, local(): call(functools.partial(rim_kernel, edge_count), (arr(*full), arr(*tile),...  4.99 us
    pallas_call x1, Pallas kernels, local(): call(inner_kernel, (arr(3, *tile), arr(*tile)), [SMEM, VMEM, VMEM, VMEM],...  4.98 us
    ppermute x1, waiting for transfers between devices, local(): far_grid = lax.ppermute(far_rows, 'band', far)  4.41 us
    pallas_call x1, Pallas kernels, local(): call(cross_kernel, arr(*full), [SMEM] * 3 + [VMEM] * 7, [pltpu.VMEM((2 *...  4.2 us
    ppermute x1, starting transfers between devices, local(): far_grid = lax.ppermute(far_rows, 'band', far)  3.02 us
    pallas_call x1, Pallas kernels, local(): call(halo_kernel, (strip, strip), [SMEM, HBM], [pltpu.SemaphoreType.DMA((...  2.72 us
    ppermute x1, waiting for transfers between devices, local(): far_norm = lax.ppermute(ac, 'band', around)  1.6 us
  transfers between devices with their start and end apart: 4, of which 2 were waited for; matrix products, arithmetic and copies ran while one was open for 0% of the time, Pallas kernels for 44%

profile of v1, /device:TPU:11, one launch (start us, length us, event | category | flops | bytes accessed | tf_op | source)
XLA Modules:
  0.0 43.2 jit_solution(15449768026203330918)
XLA Ops:
  0.0 0.0 copy-start.4
  0.0 0.0 slice-start
  0.0 2.7 %halo.1 = (bf16[384,1024]{1,0:T(8,128)(2,1)}, bf16[384,1024]{1,0:T(8,128)(2,1)}) custom-call(s32[1]{0:T(128)} %bitcast.side_ref, bf16[3072,1024]{1,0:T(8,128)(2,1)} %x_hbm.5), custom_call_target="tpu_custom_call" | custom-call | flops 10000000000 | bytes 30000000 | tf_op jit(solution)/shard_map/halo/pallas_call | solution.py:435
  2.7 0.7 %collective-permute-start = (bf16[384,1024]{1,0:T(8,128)(2,1)}, bf16[384,1024]{1,0:T(8,128)(2,1)S(1)}, u32[]{:S(2)}, u32[]{:S(2)}) collective-permute-start(bf16[384,1024]{1,0:T(8,128)(2,1)} %get-tuple-element.16), channel_id=1, source_target_pairs={{0,1},{1,0},{2,3},{3,2},{4,5},{5,4},{6,7},{7,6},{8,9},{9,8},{10,11... | collective-permute-start | bytes 2359304 | tf_op jit(solution)/shard_map/ppermute | solution.py:440
  3.5 3.0 %collective-permute-start.1 = (bf16[384,1024]{1,0:T(8,128)(2,1)}, bf16[384,1024]{1,0:T(8,128)(2,1)}, u32[]{:S(2)}, u32[]{:S(2)}) collective-permute-start(bf16[384,1024]{1,0:T(8,128)(2,1)} %get-tuple-element.17), channel_id=1, source_target_pairs={{1,2},{2,1},{3,4},{4,3},{5,6},{6,5},{7,8},{8,7},{9,10},{10,9},{11,... | collective-permute-start | bytes 2359304 | tf_op jit(solution)/shard_map/ppermute | solution.py:439
  7.2 0.0 copy-done.4
  7.2 0.0 copy-done.1
  7.2 0.0 copy-done.2
  7.2 0.0 slice-start.1
  7.2 14.2 %interior.1 = (bf16[256,1024]{1,0:T(8,128)(2,1)S(1)}, bf16[128,1024]{1,0:T(8,128)(2,1)S(1)}, bf16[128,1024]{1,0:T(8,128)(2,1)S(1)}, bf16[2,256,1024]{2,1,0:T(8,128)(2,1)}) custom-call(s32[1]{0:T(128)S(6)} %copy.18.shift_ref, s32[16,256]{1,0:T(8,128)S(1)} %pad.4.edge_ref, bf16[3072,1024]{1,0:T(8,128)(2,1)} %x_hbm.5, bf16[256,1024]{1,0:T(8,128)(2,1)S(1)} %copy-done.1, ...), custom_call_target="tpu_custom_call" | custom-call | flops 10000000000 | bytes 30000000 | tf_op jit(solution)/shard_map/interior/pallas_call | solution.py:452
  21.4 0.0 collective-permute-done.near_ref
  21.4 4.4 %collective-permute-done.1.far_ref = bf16[384,1024]{1,0:T(8,128)(2,1)} collective-permute-done((bf16[384,1024]{1,0:T(8,128)(2,1)}, bf16[384,1024]{1,0:T(8,128)(2,1)}, u32[]{:S(2)}, u32[]{:S(2)}) %collective-permute-start.1) | collective-permute-done | bytes 786464 | tf_op jit(solution)/shard_map/ppermute | solution.py:439
  25.8 5.0 %rims.1 = (bf16[256,1024]{1,0:T(8,128)(2,1)S(1)}, bf16[128,1024]{1,0:T(8,128)(2,1)S(1)}, bf16[128,1024]{1,0:T(8,128)(2,1)S(1)}) custom-call(s32[1]{0:T(128)} %bitcast.side_ref, s32[1]{0:T(128)S(6)} %copy.18.shift_ref, s32[16,256]{1,0:T(8,128)S(1)} %pad.4.edge_ref, ...), custom_call_target="tpu_custom_call", output_to_operand_aliasing={{0}: (11, {}), {1}: (12, {}), {2}: (13, {})} | custom-call | flops 1000000000 | bytes 10000000 | tf_op jit(solution)/shard_map/rims/pallas_call | solution.py:474
  30.8 0.0 copy-start
  30.8 1.5 %collective-permute-start.3 = (bf16[128,1024]{1,0:T(8,128)(2,1)S(1)}, bf16[128,1024]{1,0:T(8,128)(2,1)S(1)}, u32[]{:S(2)}, u32[]{:S(2)}) collective-permute-start(bf16[128,1024]{1,0:T(8,128)(2,1)S(1)} %get-tuple-element.22.ac_ref), channel_id=1, source_target_pairs={{1,2},{2,1},{3,4},{4,3},{5,6},{6,5},{7,8},{8,7},{9,10},{10,9},{11,... | collective-permute-start | bytes 786440 | tf_op jit(solution)/shard_map/ppermute | solution.py:493
  32.3 0.0 collective-permute-start.2
  32.3 0.0 slice-done
  32.3 0.0 slice-done.1
  32.3 0.0 copy-done.3
  32.4 5.0 %inner.1 = (bf16[3,128,1024]{2,1,0:T(8,128)(2,1)S(1)}, bf16[128,1024]{1,0:T(8,128)(2,1)S(1)}) custom-call(f32[16]{0:T(128)S(1)} %copy-done.3, bf16[128,1024]{1,0:T(8,128)(2,1)S(1)} %get-tuple-element.22.ac_ref, bf16[128,1024]{1,0:T(8,128)(2,1)S(1)} %get-tuple-element.23.b_ref, bf16[1024,3072]{1,0:T(8,128)(2,1)S(1)} %bitcast.5), custom_call_target="tpu_custom_call" | custom-call | flops 2000000000 | bytes 10000000 | tf_op jit(solution)/shard_map/inner/pallas_call | solution.py:496
  37.3 1.6 %collective-permute-done.3.far_ref = bf16[128,1024]{1,0:T(8,128)(2,1)S(1)} collective-permute-done((bf16[128,1024]{1,0:T(8,128)(2,1)S(1)}, bf16[128,1024]{1,0:T(8,128)(2,1)S(1)}, u32[]{:S(2)}, u32[]{:S(2)}) %collective-permute-start.3) | collective-permute-done | bytes 262176 | tf_op jit(solution)/shard_map/ppermute | solution.py:493
  38.9 0.0 collective-permute-done.2.near_ref
  38.9 0.0 copy-done
  38.9 4.2 %cross.1 = bf16[256,1024]{1,0:T(8,128)(2,1)} custom-call(f32[16]{0:T(128)S(1)} %copy-done.3, s32[1]{0:T(128)} %bitcast.side_ref, s32[1]{0:T(128)S(6)} %copy.18.shift_ref, bf16[128,1024]{1,0:T(8,128)(2,1)S(1)} %collective-permute-done.2.near_ref, bf16[128,1024]{1,0:T(8,128)(2,1)S(1)} %collective-permute-done.3.far_ref, ...), custom_call_target="tpu_custom_call" | custom-call | flops 2000000000 | bytes 10000000 | tf_op jit(solution)/shard_map/cross/pallas_call | solution.py:504
  (6 shorter events, 0.0 us)
Async XLA Ops:
  0.0 7.2 %copy-start.4 = (s32[256,12]{0,1:T(8,128)S(1)}, s32[256,12]{0,1:T(8,128)}, u32[]{:S(2)}) copy-start(s32[256,12]{0,1:T(8,128)} %param.13) | copy-start | bytes 36868
  0.0 7.2 %copy-start.1 = (bf16[256,1024]{1,0:T(8,128)(2,1)S(1)}, bf16[256,1024]{1,0:T(8,128)(2,1)}, u32[]{:S(2)}) copy-start(bf16[256,1024]{1,0:T(8,128)(2,1)} %mesh_ref.3) | copy-start | bytes 1572868
  0.0 7.2 %copy-start.2 = (f32[1024]{0:T(1024)S(1)}, f32[1024]{0:T(1024)}, u32[]{:S(2)}) copy-start(f32[1024]{0:T(1024)} %param.18) | copy-start | bytes 12292
  0.0 32.3 %slice-start = ((s8[6291456]{0:T(1024)(128)(4,1)}), s8[2097152]{0:T(1024)(128)(4,1)S(1)}, s32[]{:S(2)}) async-start(s8[6291456]{0:T(1024)(128)(4,1)} %bitcast.4), calls=%async_computation | async-start | bytes 4194304
  2.7 18.7 %collective-permute-start = (bf16[384,1024]{1,0:T(8,128)(2,1)}, bf16[384,1024]{1,0:T(8,128)(2,1)S(1)}, u32[]{:S(2)}, u32[]{:S(2)}) collective-permute-start(bf16[384,1024]{1,0:T(8,128)(2,1)} %get-tuple-element.16), channel_id=1, source_target_pairs={{0,1},{1,0},{2,3},{3,2},{4,5},{5,4},{6,7},{7,6},{8,9},{9,8},{10,11... | collective-permute-start | bytes 2359304 | tf_op jit(solution)/shard_map/ppermute | solution.py:440
  3.5 22.3 %collective-permute-start.1 = (bf16[384,1024]{1,0:T(8,128)(2,1)}, bf16[384,1024]{1,0:T(8,128)(2,1)}, u32[]{:S(2)}, u32[]{:S(2)}) collective-permute-start(bf16[384,1024]{1,0:T(8,128)(2,1)} %get-tuple-element.17), channel_id=1, source_target_pairs={{1,2},{2,1},{3,4},{4,3},{5,6},{6,5},{7,8},{8,7},{9,10},{10,9},{11,... | collective-permute-start | bytes 2359304 | tf_op jit(solution)/shard_map/ppermute | solution.py:439
  7.2 25.1 %slice-start.1 = ((s8[6291456]{0:T(1024)(128)(4,1)}), s8[4194304]{0:T(1024)(128)(4,1)S(1)}, s32[]{:S(2)}) async-start(s8[6291456]{0:T(1024)(128)(4,1)} %bitcast.4), calls=%async_computation.1 | async-start | bytes 8388608
  25.8 6.5 %copy-start.3 = (f32[16]{0:T(128)S(1)}, f32[16]{0:T(128)}, u32[]{:S(2)}) copy-start(f32[16]{0:T(128)} %scale_ref.3) | copy-start | bytes 196
  30.8 8.1 %copy-start = (bf16[1024,1024]{1,0:T(8,128)(2,1)S(1)}, bf16[1024,1024]{1,0:T(8,128)(2,1)}, u32[]{:S(2)}) copy-start(bf16[1024,1024]{1,0:T(8,128)(2,1)} %wo_ref.1) | copy-start | bytes 6291460
  30.8 8.1 %collective-permute-start.3 = (bf16[128,1024]{1,0:T(8,128)(2,1)S(1)}, bf16[128,1024]{1,0:T(8,128)(2,1)S(1)}, u32[]{:S(2)}, u32[]{:S(2)}) collective-permute-start(bf16[128,1024]{1,0:T(8,128)(2,1)S(1)} %get-tuple-element.22.ac_ref), channel_id=1, source_target_pairs={{1,2},{2,1},{3,4},{4,3},{5,6},{6,5},{7,8},{8,7},{9,10},{10,9},{11,... | collective-permute-start | bytes 786440 | tf_op jit(solution)/shard_map/ppermute | solution.py:493
  32.3 6.6 %collective-permute-start.2 = (bf16[128,1024]{1,0:T(8,128)(2,1)S(1)}, bf16[128,1024]{1,0:T(8,128)(2,1)S(1)}, u32[]{:S(2)}, u32[]{:S(2)}) collective-permute-start(bf16[128,1024]{1,0:T(8,128)(2,1)S(1)} %get-tuple-element.22.ac_ref), channel_id=1, source_target_pairs={{0,1},{1,0},{2,3},{3,2},{4,5},{5,4},{6,7},{7,6},{8,9},{9,8},{10,11... | collective-permute-start | bytes 786440 | tf_op jit(solution)/shard_map/ppermute | solution.py:494

commit v2 on v1

--- a/solution.py
+++ b/solution.py
@@ -103,21 +103,25 @@
     out_ref[:, cols] = total.astype(BF16)
 
 
-def halo_kernel(side_ref, x_hbm, near_ref, far_ref, sems):
-    rows = near_ref.shape[0]
+def halo_kernel(side_ref, x_hbm, near_hbm, far_hbm, held, in_sems, out_sems):
+    rows = near_hbm.shape[0]
     tail = x_hbm.shape[0] - rows
     near_at = jnp.where(side_ref[0] == 0, tail, 0)
-    copies = []
-    for i, (at, target) in enumerate(((tail - near_at, far_ref), (near_at, near_ref))):
+    fetches, sends = [], []
+    for i, (at, target) in enumerate(((tail - near_at, far_hbm), (near_at, near_hbm))):
         for k in range(rows // WIN):
+            n = i * (rows // WIN) + k
             place = pl.ds(pl.multiple_of(at + k * WIN, WIN), WIN)
-            sem = sems.at[i * (rows // WIN) + k]
             target_rows = target.at[pl.ds(k * WIN, WIN)]
-            copies.append(pltpu.make_async_copy(x_hbm.at[place], target_rows, sem))
-    for copy in copies:
-        copy.start()
-    for copy in copies:
-        copy.wait()
+            fetches.append(pltpu.make_async_copy(x_hbm.at[place], held.at[n], in_sems.at[n]))
+            sends.append(pltpu.make_async_copy(held.at[n], target_rows, out_sems.at[n]))
+    for fetch in fetches:
+        fetch.start()
+    for fetch, send in zip(fetches, sends):
+        fetch.wait()
+        send.start()
+    for send in sends:
+        send.wait()
 
 
 def interior_kernel(
@@ -227,41 +231,37 @@
 
 
 def rim_kernel(
-    edge_count, side_ref, shift_ref, edge_ref, near_ref, far_ref, x_hbm, qrim_ref, mesh_ref, wkv_hbm, we_hbm,
+    edge_count, side_ref, shift_ref, edge_ref, near_hbm, far_hbm, x_hbm, qrim_hbm, mesh_ref, wkv_hbm, we_hbm,
     gain_ref, mid_in, ac_in, b_in,
     mid_ref, ac_ref, b_ref,
-    held_low, held_high, wv_ref, we_ref, pool, gathered, total_ref, sems,
+    held, qrim_ref, wv_ref, we_ref, pool, gathered, total_ref, sems,
 ):
     mesh_rows, width = mid_ref.shape
-    get_wv = pltpu.make_async_copy(wkv_hbm.at[:, pl.ds(width, width)], wv_ref, sems.at[2])
-    get_we = pltpu.make_async_copy(we_hbm, we_ref, sems.at[3])
+    get_wv = pltpu.make_async_copy(wkv_hbm.at[:, pl.ds(width, width)], wv_ref, sems.at[5])
+    get_we = pltpu.make_async_copy(we_hbm, we_ref, sems.at[6])
     grid_rows = x_hbm.shape[0]
     heads = pool.shape[0]
     quads = width // QUAD
     wide = REACH + WIN
     tail = grid_rows - WIN
-    near_low = pltpu.make_async_copy(
-        x_hbm.at[pl.ds(0, WIN)], held_low.at[pl.ds(REACH, WIN)], sems.at[0]
-    )
-    near_low.start()
-    near_high = pltpu.make_async_copy(
-        x_hbm.at[pl.ds(tail, WIN)], held_high.at[pl.ds(tail, WIN)], sems.at[1]
-    )
-    near_high.start()
+    held_low, held_high = held.at[0], held.at[1]
+    side = side_ref[0]
+    copies = [
+        pltpu.make_async_copy(qrim_hbm, qrim_ref, sems.at[0]),
+        pltpu.make_async_copy(
+            x_hbm.at[pl.ds(0, WIN)], held_low.at[pl.ds(REACH, WIN)], sems.at[1]
+        ),
+        pltpu.make_async_copy(
+            x_hbm.at[pl.ds(tail, WIN)], held_high.at[pl.ds(tail, WIN)], sems.at[2]
+        ),
+    ]
+    for i, (end, source) in enumerate(((side, far_hbm), (1 - side, near_hbm))):
+        rows = pl.ds(pl.multiple_of(end * grid_rows, WIN), REACH)
+        copies.append(pltpu.make_async_copy(source, held.at[end, rows], sems.at[3 + i]))
+    for copy in copies:
+        copy.start()
     get_wv.start()
     get_we.start()
-    even = side_ref[0] == 0
-
-    @pl.when(even)
-    def _():
-        held_low[:REACH] = far_ref[...]
-        held_high[grid_rows:] = near_ref[...]
-
-    @pl.when(jnp.logical_not(even))
-    def _():
-        held_low[:REACH] = near_ref[...]
-        held_high[grid_rows:] = far_ref[...]
-
     rel = edge_ref[...].astype(F32).T
     rel_low = rel[:RIM, :edge_count] + float(REACH)
     rel_high = rel[mesh_rows - RIM :, :edge_count]
@@ -269,8 +269,8 @@
     count_high = count_edges(rel_high, tail, wide)
     fits = jnp.max(rel_low) < wide
     fits_high = jnp.min(rel_high) >= tail
-    near_low.wait()
-    near_high.wait()
+    for copy in copies:
+        copy.wait()
 
     def put(side, part):
         pool[:, side * RIM : (side + 1) * RIM, :] = part.reshape(heads, RIM, width)
@@ -298,6 +298,11 @@
     edge_mesh = jnp.concatenate([mesh_ref[:RIM], mesh_ref[mesh_rows - RIM :]], axis=0)
     rim_mid = (edge_mesh.astype(F32) + dot(gathered[...], we_ref[...])).astype(BF16)
     rim_norm = layer_norm(rim_mid, gain_ref[...])
+    inside = slice(RIM, mesh_rows - RIM)
+    mid_ref[inside] = mid_in[inside]
+    inside = slice(RIM, WIN - RIM)
+    ac_ref[inside] = ac_in[inside]
+    b_ref[inside] = b_in[inside]
     row = lax.broadcasted_iota(jnp.int32, (RIM, width), 0)
     for side in range(2):
         part = slice(side * RIM, (side + 1) * RIM)
@@ -334,7 +339,9 @@
     return jnp.where(second, wide[rows:], wide[:rows]).astype(BF16)
 
 
-def inner_kernel(scale_ref, ac_ref, b_ref, w_ref, ac_out, out_ref, qkv):
+def inner_kernel(
+    scale_ref, shift_ref, ac_ref, b_ref, mid_ref, w_ref, wo_ref, ac_out, mixed_ref, qkv, out
+):
     width = ac_ref.shape[1]
     rows = jnp.concatenate([ac_ref[...], b_ref[...]], axis=0)
     for n in range(width // QUAD):
@@ -348,44 +355,49 @@
             cols = slice(pair * LANES, (pair + 1) * LANES)
             scores = dot_t(pair_queries(qkv[0, :, cols]), qkv[1, :, cols])
             probs = soft_rows(scores * pair_scale(scale_ref, pair, scores.shape))
-            out_ref[:, cols] = join_pair(dot(probs, qkv[2, :, cols]))
+            out[:, cols] = join_pair(dot(probs, qkv[2, :, cols]))
+    first = lax.broadcasted_iota(jnp.int32, (WIN, QUAD), 0) < shift_ref[0]
+    for n in range(width // QUAD):
+        some = slice(n * QUAD, (n + 1) * QUAD)
+        mid = jnp.where(first, mid_ref[WIN:, some], mid_ref[:WIN, some])
+        mixed_ref[:, some] = (mid.astype(F32) + dot(out[...], wo_ref[:, some])).astype(BF16)
 
 
 def cross_kernel(
     scale_ref, side_ref, shift_ref, near_ref, far_ref, ac_ref, inner_ref, mid_ref, w_ref, wo_ref,
-    mixed_ref, keys, values, out0,
+    mixed_ref, keys, values, out,
 ):
     width = mid_ref.shape[1]
     shift = shift_ref[0]
     first = (lax.broadcasted_iota(jnp.int32, (WIN, width), 0) < shift).astype(jnp.int32)
     halo = jnp.where(first != side_ref[0], near_ref[...], far_ref[...])
-    upper = lax.broadcasted_iota(jnp.int32, (WIN, QUAD), 0) < shift
     early = lax.broadcasted_iota(jnp.int32, (2 * WIN, WIN), 0) % WIN < shift
+    early_key = lax.broadcasted_iota(jnp.int32, (2 * WIN, WIN), 1) < shift
+    owned = early.astype(jnp.int32) == early_key.astype(jnp.int32)
     zero = BF16(0)
     for n in range(width // QUAD):
         some = slice(n * QUAD, (n + 1) * QUAD)
-        for c, held in enumerate((keys, values)):
+        for c, all_rows in enumerate((keys, values)):
             at = (c + 1) * width + n * QUAD
-            part = dot(halo, w_ref[:, at : at + QUAD]).astype(BF16)
-            own = ac_ref[c + 1, :, some]
-            held[:WIN, some] = jnp.where(upper, own, part)
-            held[WIN:, some] = jnp.where(upper, part, own)
+            all_rows[:WIN, some] = ac_ref[c + 1, :, some]
+            all_rows[WIN:, some] = dot(halo, w_ref[:, at : at + QUAD]).astype(BF16)
         for pair in range(n * QUAD // LANES, (n + 1) * QUAD // LANES):
             cols = slice(pair * LANES, (pair + 1) * LANES)
             both = dot_t(pair_queries(ac_ref[0, :, cols]), keys[:, cols])
-            scores = jnp.where(early, both[:, :WIN], both[:, WIN:])
+            scores = jnp.where(owned, both[:, :WIN], both[:, WIN:])
             probs = soft_rows(scores * pair_scale(scale_ref, pair, scores.shape))
             wide = jnp.concatenate(
-                [jnp.where(early, probs, zero), jnp.where(early, zero, probs)], axis=1
+                [jnp.where(owned, probs, zero), jnp.where(owned, zero, probs)], axis=1
             )
-            part = join_pair(dot(wide, values[:, cols]))
-            inner = inner_ref[:, cols]
-            out0[:WIN, cols] = jnp.where(early[:WIN], part, inner)
-            out0[WIN:, cols] = jnp.where(early[:WIN], inner, part)
+            out[:, cols] = join_pair(dot(wide, values[:, cols]))
+    upper = lax.broadcasted_iota(jnp.int32, (WIN, QUAD), 0) < shift
     for n in range(width // QUAD):
         some = slice(n * QUAD, (n + 1) * QUAD)
-        total = mid_ref[:, some].astype(F32) + dot(out0[...], wo_ref[:, some])
-        mixed_ref[:, some] = total.astype(BF16)
+        mid = jnp.where(upper, mid_ref[:WIN, some], mid_ref[WIN:, some])
+        mixed = (mid.astype(F32) + dot(out[...], wo_ref[:, some])).astype(BF16)
+        inner = inner_ref[:, some]
+        mixed_ref[:WIN, some] = jnp.where(upper, mixed, inner)
+        mixed_ref[WIN:, some] = jnp.where(upper, inner, mixed)
 
 
 VMEM = pl.BlockSpec(memory_space=pltpu.VMEM)
@@ -394,14 +406,13 @@
 HBM = pl.BlockSpec(memory_space=pltpu.HBM)
 
 
-def call(kernel, out_shape, in_specs, scratch, mib, flops, moved, name, aliases={}):
+def call(kernel, out_shape, in_specs, scratch, mib, flops, moved, name, space=None):
     return pl.pallas_call(
         kernel,
         out_shape=out_shape,
         in_specs=in_specs,
-        out_specs=jax.tree.map(lambda _: VMEM, out_shape),
+        out_specs=jax.tree.map(lambda _: space or VMEM, out_shape),
         scratch_shapes=scratch,
-        input_output_aliases=aliases,
         compiler_params=pltpu.CompilerParams(vmem_limit_bytes=mib * 2**20),
         cost_estimate=pl.CostEstimate(flops=flops, bytes_accessed=moved, transcendentals=0),
         name=name,
@@ -434,7 +445,12 @@
     strip = jax.ShapeDtypeStruct((REACH, width), BF16)
     near_rows, far_rows = call(
         halo_kernel, (strip, strip), [SMEM, HBM],
-        [pltpu.SemaphoreType.DMA((2 * REACH // WIN,))], 57, HALO_FLOPS, HALO_BYTES, "halo",
+        [
+            pltpu.VMEM((2 * REACH // WIN, WIN, width), BF16),
+            pltpu.SemaphoreType.DMA((2 * REACH // WIN,)),
+            pltpu.SemaphoreType.DMA((2 * REACH // WIN,)),
+        ],
+        57, HALO_FLOPS, HALO_BYTES, "halo", HBM,
     )(side, grid_features)
     far_grid = lax.ppermute(far_rows, "band", far)
     near_grid = lax.ppermute(near_rows, "band", near)
@@ -470,21 +486,21 @@
         52, 10**10, 3 * 10**7, "interior",
     )(window_shift, rel, grid_features, mesh_features, w_query, w_grid_kv, w_enc_out, gain)
 
-    held = pltpu.VMEM((grid_rows + REACH, width), BF16)
     mid, ac, b = call(
         functools.partial(rim_kernel, edge_count),
         (arr(*full), arr(*tile), arr(*tile)),
-        [SMEM, SMEM, VMEM, VMEM, VMEM, HBM, VMEM, VMEM, HBM, HBM] + [VMEM] * 4,
+        [SMEM, SMEM, VMEM, ANY, ANY, HBM, ANY, VMEM, HBM, HBM] + [VMEM] * 4,
         [
-            held, held,
+            pltpu.VMEM((2, grid_rows + REACH, width), BF16),
+            pltpu.VMEM((2, heads * RIM, width), BF16),
             pltpu.VMEM((width, width), BF16),
             pltpu.VMEM((width, width), BF16),
             pltpu.VMEM((heads, 2 * RIM, width), BF16),
             pltpu.VMEM((2 * RIM, width), BF16),
             total,
-            pltpu.SemaphoreType.DMA((4,)),
+            pltpu.SemaphoreType.DMA((7,)),
         ],
-        50, 10**9, 10**7, "rims", {11: 0, 12: 1, 13: 2},
+        50, 10**9, 10**7, "rims",
     )(
         side, window_shift, rel, near_grid, far_grid, grid_features, qrim, mesh_features,
         w_grid_kv, w_enc_out, gain, mid, ac, b,
@@ -496,10 +512,10 @@
     qkv_ac, inner = call(
         inner_kernel,
         (arr(3, *tile), arr(*tile)),
-        [SMEM, VMEM, VMEM, VMEM],
-        [pltpu.VMEM((3, *tile), BF16)],
+        [SMEM, SMEM] + [VMEM] * 5,
+        [pltpu.VMEM((3, *tile), BF16), pltpu.VMEM(tile, BF16)],
         16, 2 * 10**9, 10**7, "inner",
-    )(head_scale, ac, b, w_win_qkv)
+    )(head_scale, window_shift, ac, b, mid, w_win_qkv, w_win_out)
 
     return call(
         cross_kernel,
@@ -508,10 +524,13 @@
         [
             pltpu.VMEM((2 * WIN, width), BF16),
             pltpu.VMEM((2 * WIN, width), BF16),
-            pltpu.VMEM(full, BF16),
+            pltpu.VMEM(tile, BF16),
         ],
         16, 2 * 10**9, 10**7, "cross",
-    )(head_scale, side, window_shift, near_norm, far_norm, qkv_ac, inner, mid, w_win_qkv, w_win_out)
+    )(
+        head_scale, side, window_shift, near_norm, far_norm, qkv_ac, inner, mid,
+        w_win_qkv, w_win_out,
+    )
 
 
 def solution(mesh):

time: 43.3 us -> 42.3 us (0.977)
  the two profiles are of different devices: /device:TPU:11 before, /device:TPU:0 now
where the time goes in v2:
time: 42.3 us; the launch traced here: 41.5 us
  Pallas kernels  30.5 us (72%)
  starting transfers between devices  10.1 us (24%)
  between operations  0.8 us (2%)
    pallas_call x1, Pallas kernels, local(): call(functools.partial(interior_kernel, edge_count), (arr(*full), arr(*ti...  14.3 us
    ppermute x1, starting transfers between devices, local(): far_norm = lax.ppermute(ac, 'band', around)  6.66 us
    pallas_call x1, Pallas kernels, local(): call(inner_kernel, (arr(3, *tile), arr(*tile)), [SMEM, SMEM] + [VMEM] * 5...  5.28 us
    pallas_call x1, Pallas kernels, local(): call(functools.partial(rim_kernel, edge_count), (arr(*full), arr(*tile),...  4.54 us
    pallas_call x1, Pallas kernels, local(): call(cross_kernel, arr(*full), [SMEM] * 3 + [VMEM] * 7, [pltpu.VMEM((2 *...  3.92 us
    pallas_call x1, Pallas kernels, local(): call(halo_kernel, (strip, strip), [SMEM, HBM], [pltpu.VMEM((2 * REACH //...  2.38 us
    ppermute x1, starting transfers between devices, local(): far_grid = lax.ppermute(far_rows, 'band', far)  1.54 us
    ppermute x1, starting transfers between devices, local(): near_norm = lax.ppermute(ac, 'band', near)  1.41 us
  transfers between devices with their start and end apart: 4, of which 0 were waited for; matrix products, arithmetic and copies ran while one was open for 0% of the time, Pallas kernels for 47%

profile of v2, /device:TPU:0, one launch (start us, length us, event | category | flops | bytes accessed | tf_op | source)
XLA Modules:
  0.0 41.5 jit_solution(11146380380321186630)
XLA Ops:
  0.0 0.0 copy-start.4
  0.0 2.4 %halo.1 = (bf16[384,1024]{1,0:T(8,128)(2,1)}, bf16[384,1024]{1,0:T(8,128)(2,1)}) custom-call(s32[1]{0:T(128)} %bitcast.side_ref, bf16[3072,1024]{1,0:T(8,128)(2,1)} %x_hbm.5), custom_call_target="tpu_custom_call" | custom-call | flops 10000000000 | bytes 30000000 | tf_op jit(solution)/shard_map/halo/pallas_call | solution.py:446
  2.4 0.5 %collective-permute-start = (bf16[384,1024]{1,0:T(8,128)(2,1)}, bf16[384,1024]{1,0:T(8,128)(2,1)S(1)}, u32[]{:S(2)}, u32[]{:S(2)}) collective-permute-start(bf16[384,1024]{1,0:T(8,128)(2,1)} %get-tuple-element.16), channel_id=1, source_target_pairs={{0,1},{1,0},{2,3},{3,2},{4,5},{5,4},{6,7},{7,6},{8,9},{9,8},{10,11... | collective-permute-start | bytes 2359304 | tf_op jit(solution)/shard_map/ppermute | solution.py:456
  2.9 1.5 %collective-permute-start.1 = (bf16[384,1024]{1,0:T(8,128)(2,1)}, bf16[384,1024]{1,0:T(8,128)(2,1)}, u32[]{:S(2)}, u32[]{:S(2)}) collective-permute-start(bf16[384,1024]{1,0:T(8,128)(2,1)} %get-tuple-element.17), channel_id=1, source_target_pairs={{1,2},{2,1},{3,4},{4,3},{5,6},{6,5},{7,8},{8,7},{9,10},{10,9},{11,... | collective-permute-start | bytes 2359304 | tf_op jit(solution)/shard_map/ppermute | solution.py:455
  5.1 0.0 copy-done.4
  5.2 0.0 copy-done.1
  5.2 0.0 copy-done.2
  5.2 0.0 slice-start.1
  5.2 14.3 %interior.1 = (bf16[256,1024]{1,0:T(8,128)(2,1)S(1)}, bf16[128,1024]{1,0:T(8,128)(2,1)S(1)}, bf16[128,1024]{1,0:T(8,128)(2,1)S(1)}, bf16[2,256,1024]{2,1,0:T(8,128)(2,1)}) custom-call(s32[1]{0:T(128)S(6)} %copy.12.shift_ref, s32[16,256]{1,0:T(8,128)S(1)} %pad.4.edge_ref, bf16[3072,1024]{1,0:T(8,128)(2,1)} %x_hbm.5, bf16[256,1024]{1,0:T(8,128)(2,1)S(1)} %copy-done.1, ...), custom_call_target="tpu_custom_call" | custom-call | flops 10000000000 | bytes 30000000 | tf_op jit(solution)/shard_map/interior/pallas_call | solution.py:468
  19.5 0.0 collective-permute-done.near_hbm
  19.6 0.0 collective-permute-done.1.far_hbm
  19.6 0.0 copy-start
  19.6 0.0 copy-start.3
  19.6 4.5 %rims.1 = (bf16[256,1024]{1,0:T(8,128)(2,1)S(1)}, bf16[128,1024]{1,0:T(8,128)(2,1)S(1)}, bf16[128,1024]{1,0:T(8,128)(2,1)S(1)}) custom-call(s32[1]{0:T(128)} %bitcast.side_ref, s32[1]{0:T(128)S(6)} %copy.12.shift_ref, s32[16,256]{1,0:T(8,128)S(1)} %pad.4.edge_ref, bf16[384,1024]{1,0:T(8,128)(2,1)S(1)} %collective-permute-done.near_hbm, ...), custom_call_target="tpu_custom_call" | custom-call | flops 1000000000 | bytes 10000000 | tf_op jit(solution)/shard_map/rims/pallas_call | solution.py:489
  24.1 6.7 %collective-permute-start.3 = (bf16[128,1024]{1,0:T(8,128)(2,1)S(1)}, bf16[128,1024]{1,0:T(8,128)(2,1)S(1)}, u32[]{:S(2)}, u32[]{:S(2)}) collective-permute-start(bf16[128,1024]{1,0:T(8,128)(2,1)S(1)} %get-tuple-element.22.ac_ref), channel_id=1, source_target_pairs={{1,2},{2,1},{3,4},{4,3},{5,6},{6,5},{7,8},{8,7},{9,10},{10,9},{11,... | collective-permute-start | bytes 786440 | tf_op jit(solution)/shard_map/ppermute | solution.py:509
  30.8 1.4 %collective-permute-start.2 = (bf16[128,1024]{1,0:T(8,128)(2,1)S(1)}, bf16[128,1024]{1,0:T(8,128)(2,1)S(1)}, u32[]{:S(2)}, u32[]{:S(2)}) collective-permute-start(bf16[128,1024]{1,0:T(8,128)(2,1)S(1)} %get-tuple-element.22.ac_ref), channel_id=1, source_target_pairs={{0,1},{1,0},{2,3},{3,2},{4,5},{5,4},{6,7},{7,6},{8,9},{9,8},{10,11... | collective-permute-start | bytes 786440 | tf_op jit(solution)/shard_map/ppermute | solution.py:510
  32.2 0.0 slice-done
  32.2 0.0 slice-done.1
  32.2 0.0 copy-done
  32.2 0.0 copy-done.3
  32.2 5.3 %inner.1 = (bf16[3,128,1024]{2,1,0:T(8,128)(2,1)S(1)}, bf16[128,1024]{1,0:T(8,128)(2,1)S(1)}) custom-call(f32[16]{0:T(128)S(1)} %copy-done.3, s32[1]{0:T(128)S(6)} %copy.12.shift_ref, bf16[128,1024]{1,0:T(8,128)(2,1)S(1)} %get-tuple-element.22.ac_ref, bf16[128,1024]{1,0:T(8,128)(2,1)S(1)} %get-tuple-element.23.b_ref, ...), custom_call_target="tpu_custom_call" | custom-call | flops 2000000000 | bytes 10000000 | tf_op jit(solution)/shard_map/inner/pallas_call | solution.py:512
  37.5 0.0 collective-permute-done.3.far_ref
  37.5 0.0 collective-permute-done.2.near_ref
  37.5 3.9 %cross.1 = bf16[256,1024]{1,0:T(8,128)(2,1)} custom-call(f32[16]{0:T(128)S(1)} %copy-done.3, s32[1]{0:T(128)} %bitcast.side_ref, s32[1]{0:T(128)S(6)} %copy.12.shift_ref, bf16[128,1024]{1,0:T(8,128)(2,1)S(1)} %collective-permute-done.2.near_ref, bf16[128,1024]{1,0:T(8,128)(2,1)S(1)} %collective-permute-done.3.far_ref, ...), custom_call_target="tpu_custom_call" | custom-call | flops 2000000000 | bytes 10000000 | tf_op jit(solution)/shard_map/cross/pallas_call | solution.py:520
  (6 shorter events, 0.0 us)
Async XLA Ops:
  0.0 5.1 %copy-start.4 = (s32[256,12]{0,1:T(8,128)S(1)}, s32[256,12]{0,1:T(8,128)}, u32[]{:S(2)}) copy-start(s32[256,12]{0,1:T(8,128)} %param.13) | copy-start | bytes 36868
  0.0 5.2 %copy-start.1 = (bf16[256,1024]{1,0:T(8,128)(2,1)S(1)}, bf16[256,1024]{1,0:T(8,128)(2,1)}, u32[]{:S(2)}) copy-start(bf16[256,1024]{1,0:T(8,128)(2,1)} %mesh_ref.3) | copy-start | bytes 1572868
  0.0 5.2 %copy-start.2 = (f32[1024]{0:T(1024)S(1)}, f32[1024]{0:T(1024)}, u32[]{:S(2)}) copy-start(f32[1024]{0:T(1024)} %param.18) | copy-start | bytes 12292
  0.0 32.2 %slice-start = ((s8[6291456]{0:T(1024)(128)(4,1)}), s8[2097152]{0:T(1024)(128)(4,1)S(1)}, s32[]{:S(2)}) async-start(s8[6291456]{0:T(1024)(128)(4,1)} %bitcast.4), calls=%async_computation | async-start | bytes 4194304
  2.4 17.1 %collective-permute-start = (bf16[384,1024]{1,0:T(8,128)(2,1)}, bf16[384,1024]{1,0:T(8,128)(2,1)S(1)}, u32[]{:S(2)}, u32[]{:S(2)}) collective-permute-start(bf16[384,1024]{1,0:T(8,128)(2,1)} %get-tuple-element.16), channel_id=1, source_target_pairs={{0,1},{1,0},{2,3},{3,2},{4,5},{5,4},{6,7},{7,6},{8,9},{9,8},{10,11... | collective-permute-start | bytes 2359304 | tf_op jit(solution)/shard_map/ppermute | solution.py:456
  2.9 16.6 %collective-permute-start.1 = (bf16[384,1024]{1,0:T(8,128)(2,1)}, bf16[384,1024]{1,0:T(8,128)(2,1)}, u32[]{:S(2)}, u32[]{:S(2)}) collective-permute-start(bf16[384,1024]{1,0:T(8,128)(2,1)} %get-tuple-element.17), channel_id=1, source_target_pairs={{1,2},{2,1},{3,4},{4,3},{5,6},{6,5},{7,8},{8,7},{9,10},{10,9},{11,... | collective-permute-start | bytes 2359304 | tf_op jit(solution)/shard_map/ppermute | solution.py:455
  5.2 27.0 %slice-start.1 = ((s8[6291456]{0:T(1024)(128)(4,1)}), s8[4194304]{0:T(1024)(128)(4,1)S(1)}, s32[]{:S(2)}) async-start(s8[6291456]{0:T(1024)(128)(4,1)} %bitcast.4), calls=%async_computation.1 | async-start | bytes 8388608
  19.6 12.7 %copy-start = (bf16[1024,1024]{1,0:T(8,128)(2,1)S(1)}, bf16[1024,1024]{1,0:T(8,128)(2,1)}, u32[]{:S(2)}) copy-start(bf16[1024,1024]{1,0:T(8,128)(2,1)} %wo_ref.3) | copy-start | bytes 6291460
  19.6 12.6 %copy-start.3 = (f32[16]{0:T(128)S(1)}, f32[16]{0:T(128)}, u32[]{:S(2)}) copy-start(f32[16]{0:T(128)} %scale_ref.3) | copy-start | bytes 196
  24.1 13.4 %collective-permute-start.3 = (bf16[128,1024]{1,0:T(8,128)(2,1)S(1)}, bf16[128,1024]{1,0:T(8,128)(2,1)S(1)}, u32[]{:S(2)}, u32[]{:S(2)}) collective-permute-start(bf16[128,1024]{1,0:T(8,128)(2,1)S(1)} %get-tuple-element.22.ac_ref), channel_id=1, source_target_pairs={{1,2},{2,1},{3,4},{4,3},{5,6},{6,5},{7,8},{8,7},{9,10},{10,9},{11,... | collective-permute-start | bytes 786440 | tf_op jit(solution)/shard_map/ppermute | solution.py:509
  30.8 6.7 %collective-permute-start.2 = (bf16[128,1024]{1,0:T(8,128)(2,1)S(1)}, bf16[128,1024]{1,0:T(8,128)(2,1)S(1)}, u32[]{:S(2)}, u32[]{:S(2)}) collective-permute-start(bf16[128,1024]{1,0:T(8,128)(2,1)S(1)} %get-tuple-element.22.ac_ref), channel_id=1, source_target_pairs={{0,1},{1,0},{2,3},{3,2},{4,5},{5,4},{6,7},{7,6},{8,9},{9,8},{10,11... | collective-permute-start | bytes 786440 | tf_op jit(solution)/shard_map/ppermute | solution.py:510

commit v3 on v2

--- a/solution.py
+++ b/solution.py
@@ -381,6 +381,7 @@
             at = (c + 1) * width + n * QUAD
             all_rows[:WIN, some] = ac_ref[c + 1, :, some]
             all_rows[WIN:, some] = dot(halo, w_ref[:, at : at + QUAD]).astype(BF16)
+    for n in range(width // QUAD):
         for pair in range(n * QUAD // LANES, (n + 1) * QUAD // LANES):
             cols = slice(pair * LANES, (pair + 1) * LANES)
             both = dot_t(pair_queries(ac_ref[0, :, cols]), keys[:, cols])

time: 42.3 us -> 42.1 us (level)
  no operation moved by 1% of the time
where the time goes in v3:
time: 42.1 us; the launch traced here: 41.3 us
  Pallas kernels  30.3 us (72%)
  starting transfers between devices  10.1 us (24%)
  between operations  0.8 us (2%)
    pallas_call x1, Pallas kernels, local(): call(functools.partial(interior_kernel, edge_count), (arr(*full), arr(*ti...  14.3 us
    ppermute x1, starting transfers between devices, local(): far_norm = lax.ppermute(ac, 'band', around)  6.66 us
    pallas_call x1, Pallas kernels, local(): call(inner_kernel, (arr(3, *tile), arr(*tile)), [SMEM, SMEM] + [VMEM] * 5...  5.28 us
    pallas_call x1, Pallas kernels, local(): call(functools.partial(rim_kernel, edge_count), (arr(*full), arr(*tile),...  4.54 us
    pallas_call x1, Pallas kernels, local(): call(cross_kernel, arr(*full), [SMEM] * 3 + [VMEM] * 7, [pltpu.VMEM((2 *...  3.74 us
    pallas_call x1, Pallas kernels, local(): call(halo_kernel, (strip, strip), [SMEM, HBM], [pltpu.VMEM((2 * REACH //...  2.38 us
    ppermute x1, starting transfers between devices, local(): far_grid = lax.ppermute(far_rows, 'band', far)  1.54 us
    ppermute x1, starting transfers between devices, local(): near_norm = lax.ppermute(ac, 'band', near)  1.41 us
  transfers between devices with their start and end apart: 4, of which 0 were waited for; matrix products, arithmetic and copies ran while one was open for 0% of the time, Pallas kernels for 47%

profile of v3, /device:TPU:0, one launch (start us, length us, event | category | flops | bytes accessed | tf_op | source)
XLA Modules:
  0.0 41.3 jit_solution(8283979254120131004)
XLA Ops:
  0.0 0.0 copy-start.4
  0.0 2.4 %halo.1 = (bf16[384,1024]{1,0:T(8,128)(2,1)}, bf16[384,1024]{1,0:T(8,128)(2,1)}) custom-call(s32[1]{0:T(128)} %bitcast.side_ref, bf16[3072,1024]{1,0:T(8,128)(2,1)} %x_hbm.5), custom_call_target="tpu_custom_call" | custom-call | flops 10000000000 | bytes 30000000 | tf_op jit(solution)/shard_map/halo/pallas_call | solution.py:447
  2.4 0.5 %collective-permute-start = (bf16[384,1024]{1,0:T(8,128)(2,1)}, bf16[384,1024]{1,0:T(8,128)(2,1)S(1)}, u32[]{:S(2)}, u32[]{:S(2)}) collective-permute-start(bf16[384,1024]{1,0:T(8,128)(2,1)} %get-tuple-element.16), channel_id=1, source_target_pairs={{0,1},{1,0},{2,3},{3,2},{4,5},{5,4},{6,7},{7,6},{8,9},{9,8},{10,11... | collective-permute-start | bytes 2359304 | tf_op jit(solution)/shard_map/ppermute | solution.py:457
  2.9 1.5 %collective-permute-start.1 = (bf16[384,1024]{1,0:T(8,128)(2,1)}, bf16[384,1024]{1,0:T(8,128)(2,1)}, u32[]{:S(2)}, u32[]{:S(2)}) collective-permute-start(bf16[384,1024]{1,0:T(8,128)(2,1)} %get-tuple-element.17), channel_id=1, source_target_pairs={{1,2},{2,1},{3,4},{4,3},{5,6},{6,5},{7,8},{8,7},{9,10},{10,9},{11,... | collective-permute-start | bytes 2359304 | tf_op jit(solution)/shard_map/ppermute | solution.py:456
  5.1 0.0 copy-done.4
  5.2 0.0 copy-done.1
  5.2 0.0 copy-done.2
  5.2 0.0 slice-start.1
  5.2 14.3 %interior.1 = (bf16[256,1024]{1,0:T(8,128)(2,1)S(1)}, bf16[128,1024]{1,0:T(8,128)(2,1)S(1)}, bf16[128,1024]{1,0:T(8,128)(2,1)S(1)}, bf16[2,256,1024]{2,1,0:T(8,128)(2,1)}) custom-call(s32[1]{0:T(128)S(6)} %copy.12.shift_ref, s32[16,256]{1,0:T(8,128)S(1)} %pad.4.edge_ref, bf16[3072,1024]{1,0:T(8,128)(2,1)} %x_hbm.5, bf16[256,1024]{1,0:T(8,128)(2,1)S(1)} %copy-done.1, ...), custom_call_target="tpu_custom_call" | custom-call | flops 10000000000 | bytes 30000000 | tf_op jit(solution)/shard_map/interior/pallas_call | solution.py:469
  19.5 0.0 collective-permute-done.near_hbm
  19.6 0.0 collective-permute-done.1.far_hbm
  19.6 0.0 copy-start
  19.6 0.0 copy-start.3
  19.6 4.5 %rims.1 = (bf16[256,1024]{1,0:T(8,128)(2,1)S(1)}, bf16[128,1024]{1,0:T(8,128)(2,1)S(1)}, bf16[128,1024]{1,0:T(8,128)(2,1)S(1)}) custom-call(s32[1]{0:T(128)} %bitcast.side_ref, s32[1]{0:T(128)S(6)} %copy.12.shift_ref, s32[16,256]{1,0:T(8,128)S(1)} %pad.4.edge_ref, bf16[384,1024]{1,0:T(8,128)(2,1)S(1)} %collective-permute-done.near_hbm, ...), custom_call_target="tpu_custom_call" | custom-call | flops 1000000000 | bytes 10000000 | tf_op jit(solution)/shard_map/rims/pallas_call | solution.py:490
  24.1 6.7 %collective-permute-start.3 = (bf16[128,1024]{1,0:T(8,128)(2,1)S(1)}, bf16[128,1024]{1,0:T(8,128)(2,1)S(1)}, u32[]{:S(2)}, u32[]{:S(2)}) collective-permute-start(bf16[128,1024]{1,0:T(8,128)(2,1)S(1)} %get-tuple-element.22.ac_ref), channel_id=1, source_target_pairs={{1,2},{2,1},{3,4},{4,3},{5,6},{6,5},{7,8},{8,7},{9,10},{10,9},{11,... | collective-permute-start | bytes 786440 | tf_op jit(solution)/shard_map/ppermute | solution.py:510
  30.8 1.4 %collective-permute-start.2 = (bf16[128,1024]{1,0:T(8,128)(2,1)S(1)}, bf16[128,1024]{1,0:T(8,128)(2,1)S(1)}, u32[]{:S(2)}, u32[]{:S(2)}) collective-permute-start(bf16[128,1024]{1,0:T(8,128)(2,1)S(1)} %get-tuple-element.22.ac_ref), channel_id=1, source_target_pairs={{0,1},{1,0},{2,3},{3,2},{4,5},{5,4},{6,7},{7,6},{8,9},{9,8},{10,11... | collective-permute-start | bytes 786440 | tf_op jit(solution)/shard_map/ppermute | solution.py:511
  32.2 0.0 slice-done
  32.2 0.0 slice-done.1
  32.2 0.0 copy-done
  32.2 0.0 copy-done.3
  32.2 5.3 %inner.1 = (bf16[3,128,1024]{2,1,0:T(8,128)(2,1)S(1)}, bf16[128,1024]{1,0:T(8,128)(2,1)S(1)}) custom-call(f32[16]{0:T(128)S(1)} %copy-done.3, s32[1]{0:T(128)S(6)} %copy.12.shift_ref, bf16[128,1024]{1,0:T(8,128)(2,1)S(1)} %get-tuple-element.22.ac_ref, bf16[128,1024]{1,0:T(8,128)(2,1)S(1)} %get-tuple-element.23.b_ref, ...), custom_call_target="tpu_custom_call" | custom-call | flops 2000000000 | bytes 10000000 | tf_op jit(solution)/shard_map/inner/pallas_call | solution.py:513
  37.5 0.0 collective-permute-done.3.far_ref
  37.5 0.0 collective-permute-done.2.near_ref
  37.5 3.7 %cross.1 = bf16[256,1024]{1,0:T(8,128)(2,1)} custom-call(f32[16]{0:T(128)S(1)} %copy-done.3, s32[1]{0:T(128)} %bitcast.side_ref, s32[1]{0:T(128)S(6)} %copy.12.shift_ref, bf16[128,1024]{1,0:T(8,128)(2,1)S(1)} %collective-permute-done.2.near_ref, bf16[128,1024]{1,0:T(8,128)(2,1)S(1)} %collective-permute-done.3.far_ref, ...), custom_call_target="tpu_custom_call" | custom-call | flops 2000000000 | bytes 10000000 | tf_op jit(solution)/shard_map/cross/pallas_call | solution.py:521
  (6 shorter events, 0.0 us)
Async XLA Ops:
  0.0 5.1 %copy-start.4 = (s32[256,12]{0,1:T(8,128)S(1)}, s32[256,12]{0,1:T(8,128)}, u32[]{:S(2)}) copy-start(s32[256,12]{0,1:T(8,128)} %param.13) | copy-start | bytes 36868
  0.0 5.2 %copy-start.1 = (bf16[256,1024]{1,0:T(8,128)(2,1)S(1)}, bf16[256,1024]{1,0:T(8,128)(2,1)}, u32[]{:S(2)}) copy-start(bf16[256,1024]{1,0:T(8,128)(2,1)} %mesh_ref.3) | copy-start | bytes 1572868
  0.0 5.2 %copy-start.2 = (f32[1024]{0:T(1024)S(1)}, f32[1024]{0:T(1024)}, u32[]{:S(2)}) copy-start(f32[1024]{0:T(1024)} %param.18) | copy-start | bytes 12292
  0.0 32.2 %slice-start = ((s8[6291456]{0:T(1024)(128)(4,1)}), s8[2097152]{0:T(1024)(128)(4,1)S(1)}, s32[]{:S(2)}) async-start(s8[6291456]{0:T(1024)(128)(4,1)} %bitcast.4), calls=%async_computation | async-start | bytes 4194304
  2.4 17.1 %collective-permute-start = (bf16[384,1024]{1,0:T(8,128)(2,1)}, bf16[384,1024]{1,0:T(8,128)(2,1)S(1)}, u32[]{:S(2)}, u32[]{:S(2)}) collective-permute-start(bf16[384,1024]{1,0:T(8,128)(2,1)} %get-tuple-element.16), channel_id=1, source_target_pairs={{0,1},{1,0},{2,3},{3,2},{4,5},{5,4},{6,7},{7,6},{8,9},{9,8},{10,11... | collective-permute-start | bytes 2359304 | tf_op jit(solution)/shard_map/ppermute | solution.py:457
  2.9 16.6 %collective-permute-start.1 = (bf16[384,1024]{1,0:T(8,128)(2,1)}, bf16[384,1024]{1,0:T(8,128)(2,1)}, u32[]{:S(2)}, u32[]{:S(2)}) collective-permute-start(bf16[384,1024]{1,0:T(8,128)(2,1)} %get-tuple-element.17), channel_id=1, source_target_pairs={{1,2},{2,1},{3,4},{4,3},{5,6},{6,5},{7,8},{8,7},{9,10},{10,9},{11,... | collective-permute-start | bytes 2359304 | tf_op jit(solution)/shard_map/ppermute | solution.py:456
  5.2 27.0 %slice-start.1 = ((s8[6291456]{0:T(1024)(128)(4,1)}), s8[4194304]{0:T(1024)(128)(4,1)S(1)}, s32[]{:S(2)}) async-start(s8[6291456]{0:T(1024)(128)(4,1)} %bitcast.4), calls=%async_computation.1 | async-start | bytes 8388608
  19.6 12.7 %copy-start = (bf16[1024,1024]{1,0:T(8,128)(2,1)S(1)}, bf16[1024,1024]{1,0:T(8,128)(2,1)}, u32[]{:S(2)}) copy-start(bf16[1024,1024]{1,0:T(8,128)(2,1)} %wo_ref.3) | copy-start | bytes 6291460
  19.6 12.6 %copy-start.3 = (f32[16]{0:T(128)S(1)}, f32[16]{0:T(128)}, u32[]{:S(2)}) copy-start(f32[16]{0:T(128)} %scale_ref.3) | copy-start | bytes 196
  24.1 13.4 %collective-permute-start.3 = (bf16[128,1024]{1,0:T(8,128)(2,1)S(1)}, bf16[128,1024]{1,0:T(8,128)(2,1)S(1)}, u32[]{:S(2)}, u32[]{:S(2)}) collective-permute-start(bf16[128,1024]{1,0:T(8,128)(2,1)S(1)} %get-tuple-element.22.ac_ref), channel_id=1, source_target_pairs={{1,2},{2,1},{3,4},{4,3},{5,6},{6,5},{7,8},{8,7},{9,10},{10,9},{11,... | collective-permute-start | bytes 786440 | tf_op jit(solution)/shard_map/ppermute | solution.py:510
  30.8 6.7 %collective-permute-start.2 = (bf16[128,1024]{1,0:T(8,128)(2,1)S(1)}, bf16[128,1024]{1,0:T(8,128)(2,1)S(1)}, u32[]{:S(2)}, u32[]{:S(2)}) collective-permute-start(bf16[128,1024]{1,0:T(8,128)(2,1)S(1)} %get-tuple-element.22.ac_ref), channel_id=1, source_target_pairs={{0,1},{1,0},{2,3},{3,2},{4,5},{5,4},{6,7},{7,6},{8,9},{9,8},{10,11... | collective-permute-start | bytes 786440 | tf_op jit(solution)/shard_map/ppermute | solution.py:511
